TPU v7x, 32 devices: a whole 2x2x4 slice. The times are simulated.
32 devices in a mesh: dp: 8 (over z, x), fsdp: 4 (over y, core).
Axes of the slice: x: 2, y: 2, z: 4, core: 2. Of those that a mesh axis runs over, the one named last changes fastest.
Arguments:
- hidden_in: bfloat16 [2, 8, 1024, 1024], P(None, 'dp', 'fsdp'), may hold values from -6 to 6
- segment_ids: int32 [2, 8, 1024], P(None, 'dp', 'fsdp'), may hold values from 0 to 1023, as said below
- norm1_gain: bfloat16 [1024], P(('dp', 'fsdp')), may hold values from 0.5 to 1.5
- w_gate_z: bfloat16 [1024, 1536], P(('dp', 'fsdp')), may hold values from -0.1875 to 0.1875
- w_xbc: bfloat16 [1024, 1792], P(('dp', 'fsdp')), may hold values from -0.1875 to 0.1875
- w_step: bfloat16 [1024, 24], P(('dp', 'fsdp')), may hold values from -0.1875 to 0.1875
- conv_weight: bfloat16 [4, 1792], P(None, ('dp', 'fsdp')), may hold values from -3 to 3
- conv_bias: bfloat16 [1792], P(('dp', 'fsdp')), may hold values from -3 to 3
- step_bias: float32 [24], replicated, may hold values from -1 to 0.5
- decay_log: float32 [24], replicated, may hold values from -12 to -2
- skip_gain: float32 [24], replicated, may hold values from 0.5 to 1.5
- mixer_gain: bfloat16 [1536], P(('dp', 'fsdp')), may hold values from 0.5 to 1.5
- w_mix_out: bfloat16 [1536, 1024], P(('dp', 'fsdp')), may hold values from -0.15625 to 0.15625
- w_query: bfloat16 [1024, 512], P(('dp', 'fsdp')), may hold values from -0.1875 to 0.1875
- key_value_weight: bfloat16 [1024, 256], P(('dp', 'fsdp')), may hold values from -0.1875 to 0.1875
- w_attn_out: bfloat16 [512, 1024], P(('dp', 'fsdp')), may hold values from -1 to 1
- norm2_gain: bfloat16 [1024], P(('dp', 'fsdp')), may hold values from 0.5 to 1.5
- w_gate_up: bfloat16 [1024, 4096], P(('dp', 'fsdp')), may hold values from -0.1875 to 0.1875
- w_down: bfloat16 [2048, 1024], P(('dp', 'fsdp')), may hold values from -0.125 to 0.125
- out_grad: bfloat16 [2, 8, 1024, 1024], P(None, 'dp', 'fsdp'), may hold values from -6 to 6
Outputs:
- hidden_out: bfloat16 [2, 8, 1024, 1024], P(None, 'dp', 'fsdp')
- input_grad: float32 [2, 8, 1024, 1024], P(None, 'dp', 'fsdp')
- grad_norm1_gain: float32 [1024], P(('dp', 'fsdp'))
- grad_w_gate_z: float32 [1024, 1536], P(('dp', 'fsdp'))
- grad_w_xbc: float32 [1024, 1792], P(('dp', 'fsdp'))
- grad_w_step: float32 [1024, 24], P(('dp', 'fsdp'))
- grad_conv_weight: float32 [4, 1792], P(None, ('dp', 'fsdp'))
- grad_conv_bias: float32 [1792], P(('dp', 'fsdp'))
- grad_step_bias: float32 [24], replicated
- grad_decay_log: float32 [24], replicated
- grad_skip_gain: float32 [24], replicated
- grad_mixer_gain: float32 [1536], P(('dp', 'fsdp'))
- grad_w_mix_out: float32 [1536, 1024], P(('dp', 'fsdp'))
- grad_w_query: float32 [1024, 512], P(('dp', 'fsdp'))
- grad_w_keyval: float32 [1024, 256], P(('dp', 'fsdp'))
- grad_w_attn_out: float32 [512, 1024], P(('dp', 'fsdp'))
- grad_norm2_gain: float32 [1024], P(('dp', 'fsdp'))
- grad_w_gate_up: float32 [1024, 4096], P(('dp', 'fsdp'))
- grad_w_down: float32 [2048, 1024], P(('dp', 'fsdp'))
Inputs may be any that keep to these rules, and one draw needn't show every extreme that they name: `segment_ids`: ids start at 0 and never fall along a sequence, and the last document of every sequence has id 1024 - 1; in every sequence one document covers 1024 - 255 or more positions.
All inputs are finite; a program needn't handle non-finite values.
Results may differ from a plain program's by a relative error of at most 0.034.
Values may be sent and summed in bfloat16 or wider, within the bound.
No kernel may reach another device: no remote copies, remote signals or barrier semaphores. Data moves between devices by JAX's collectives and lax.ppermute only.
A program may use at most 256 MiB of HBM per device.

v0:
```python
import jax
import jax.numpy as jnp
from jax import lax
from jax.sharding import PartitionSpec as P

MODEL_WIDTH = 1024
FF = 2048
H = 24
P_SIZE = 64
NS = 128
QUERY_HEADS = 8
KEY_VALUE_HEADS = 2
HEAD_WIDTH = 64
KC = 4
MB = 2
DI = 1536


EPSILON = 1e-06
NEGATIVE = -1e30
HIGHEST = lax.Precision.HIGHEST


def from_behind(block, axis, distance):
    devices = range(lax.axis_size(axis))
    route = [(i - distance, i) for i in devices if i - distance in devices]
    return lax.ppermute(block, axis, route)


def entering(value, axis, join, neutral):
    place = lax.axis_index(axis)
    gathered = jax.tree.map(
        lambda a, kind: lax.all_gather(a.astype(kind), axis),
        value,
        (jnp.bfloat16, jnp.bfloat16, jnp.int32, jnp.int32),
    )
    state = jax.tree.map(lambda a, e: jnp.zeros_like(a) + jnp.asarray(e, a.dtype), value, neutral)

    def one(step, state):
        return join(
            state,
            jax.tree.map(
                lambda a, own: lax.dynamic_index_in_dim(a, step, 0, False).astype(own.dtype),
                gathered,
                value,
            ),
        )

    return lax.fori_loop(0, place, one, state)


def entering_2(value, axis, join, neutral):
    count = lax.axis_size(axis)
    place = lax.axis_index(axis)
    ahead = count - 1 - place
    gathered = jax.tree.map(
        lambda a, kind: lax.all_gather(a.astype(kind), axis),
        value,
        jax.tree.map(lambda a: jnp.bfloat16 if a.dtype == jnp.float32 else a.dtype, value),
    )
    state = jax.tree.map(lambda a, e: jnp.zeros_like(a) + jnp.asarray(e, a.dtype), value, neutral)

    def one(step, state):
        source = count - 1 - step
        return join(
            state,
            jax.tree.map(
                lambda a, own: lax.dynamic_index_in_dim(a, source, 0, False).astype(own.dtype),
                gathered,
                value,
            ),
        )

    return lax.fori_loop(0, ahead, one, state)


def matmul(first_op, second_op):
    return jnp.dot(first_op, second_op, preferred_element_type=jnp.float32)


def left_t(first_op, second_op):
    return jnp.einsum("ti,tj->ij", first_op, second_op, preferred_element_type=jnp.float32)


def right_t(first_op, second_op):
    return jnp.einsum("ti,ji->tj", first_op, second_op, preferred_element_type=jnp.float32)


def rms_gain(values, gain_in):
    return values * lax.rsqrt(jnp.mean(values * values, axis=-1, keepdims=True) + EPSILON) * gain_in


def conv_mix(extended, seg_ext, kernel, offset):
    sequence_length = extended.shape[0] - (KC - 1)
    summed = jnp.zeros((sequence_length, extended.shape[1]), jnp.float32) + offset[None, :]
    for tap_index in range(KC):
        same_doc = (seg_ext[tap_index : tap_index + sequence_length] == seg_ext[KC - 1 :]).astype(
            jnp.float32
        )
        summed = (
            summed
            + kernel[tap_index][None, :]
            * extended[tap_index : tap_index + sequence_length]
            * same_doc[:, None]
        )
    return jax.nn.silu(summed)


def split_parts(conv_out):
    sequence_length = conv_out.shape[0]
    inputs = conv_out[:, : H * P_SIZE].reshape(sequence_length, H, P_SIZE)
    b_rows = conv_out[:, H * P_SIZE : H * P_SIZE + NS]
    c_rows = conv_out[:, H * P_SIZE + NS :]
    return (inputs, b_rows, c_rows)


def decay_terms(raw_step, step_bias, decay_log):
    step_size = jax.nn.softplus(raw_step + step_bias[None, :])
    cumulated = jnp.cumsum(-step_size * jnp.exp(decay_log)[None, :], axis=0)
    return (step_size, cumulated)


def state_local(conv_out, raw_step, step_bias, decay_log, seg_ids):
    inputs, b_rows, c_rows = split_parts(conv_out)
    step_size, cumulated = decay_terms(raw_step, step_bias, decay_log)
    keep_end = (seg_ids == seg_ids[-1]).astype(jnp.float32)
    weight_set = jnp.exp(cumulated[-1][None, :] - cumulated) * step_size * keep_end[:, None]
    weighted = inputs * weight_set[:, :, None]
    end_state = jnp.einsum("shp,sn->hpn", weighted, b_rows, precision=HIGHEST)
    carry_gate = jnp.exp(cumulated[-1]) * (seg_ids[0] == seg_ids[-1]).astype(jnp.float32)
    return (end_state, carry_gate)


def mixer_output(
    conv_out, raw_step, step_bias, decay_log, skip_gain, seg_ids, prev_state, prev_last
):
    inputs, b_rows, c_rows = split_parts(conv_out)
    step_size, cumulated = decay_terms(raw_step, step_bias, decay_log)
    sequence_length = conv_out.shape[0]
    places = lax.iota(jnp.int32, sequence_length)
    allowed = (seg_ids[:, None] == seg_ids[None, :]) & (places[:, None] >= places[None, :])
    by_head = cumulated.T
    spread = jnp.where(allowed[None], by_head[:, :, None] - by_head[:, None, :], NEGATIVE)
    couple = jnp.dot(c_rows, b_rows.T, precision=HIGHEST, preferred_element_type=jnp.float32)
    mixing = jnp.exp(spread) * couple[None] * step_size.T[:, None, :]
    inside = jnp.einsum("hts,shp->thp", mixing, inputs, precision=HIGHEST)
    inflow = jnp.exp(cumulated) * (seg_ids == prev_last).astype(jnp.float32)[:, None]
    carried = jnp.einsum("tn,hpn->thp", c_rows, prev_state, precision=HIGHEST) * inflow[:, :, None]
    result = inside + carried + skip_gain[None, :, None] * inputs
    return result.reshape(sequence_length, H * P_SIZE)


def gated_norm(mixer_out, gate_in, gain_in):
    return rms_gain(mixer_out * jax.nn.silu(gate_in), gain_in)


def swiglu(gate_up):
    return jax.nn.silu(gate_up[:, :FF]) * gate_up[:, FF:]


def join_states(earlier, later_in):
    gate_early, state_early, first_early, last_early = earlier
    gate_late, state_late, first_late, last_late = later_in
    linked = ((last_early == first_late) | (last_early < 0) | (first_late < 0)).astype(jnp.float32)
    through = gate_late * linked
    return (
        gate_early * through,
        state_late + through[:, None, None] * state_early,
        jnp.where(first_early < 0, first_late, first_early),
        jnp.where(last_late < 0, last_early, last_late),
    )


def join_back(earlier, later_in):
    gate_early, grad_early = earlier
    gate_late, grad_late = later_in
    return (gate_early * gate_late, grad_late + gate_late[:, None, None] * grad_early)


def head_scores(query_head_rows, segment_key_value, piece_seg, query_pos, query_seg):
    segment_length = segment_key_value.shape[0]
    local_rows = query_head_rows.shape[0]
    head_groups = QUERY_HEADS // KEY_VALUE_HEADS
    segment_key_rows = segment_key_value[:, : KEY_VALUE_HEADS * HEAD_WIDTH].reshape(
        segment_length, KEY_VALUE_HEADS, HEAD_WIDTH
    )
    segment_value_rows = segment_key_value[:, KEY_VALUE_HEADS * HEAD_WIDTH :].reshape(
        segment_length, KEY_VALUE_HEADS, HEAD_WIDTH
    )
    key_pos = lax.iota(jnp.int32, segment_length)
    allowed = (piece_seg[None, :] == query_seg[:, None]) & (key_pos[None, :] <= query_pos[:, None])
    grouped_heads = query_head_rows.reshape(local_rows, KEY_VALUE_HEADS, head_groups, HEAD_WIDTH)
    scores = jnp.einsum(
        "qgjd,kgd->gjqk", grouped_heads, segment_key_rows, preferred_element_type=jnp.float32
    ) * HEAD_WIDTH ** (-0.5)
    scores = jnp.where(
        allowed[None], scores.reshape(QUERY_HEADS, local_rows, segment_length), NEGATIVE
    )
    return (scores, allowed, segment_key_rows, segment_value_rows, grouped_heads)


def mixer_forward(conv_seq, seg_ids, raw_seq, kernel_f, offset_f, step_bias, decay_log, skip_gain):
    local_rows = conv_seq.shape[0]
    halo_rows = KC - 1
    prev_rows, prev_ids = from_behind(
        (conv_seq[local_rows - halo_rows :], seg_ids[local_rows - halo_rows :]), "fsdp", 1
    )
    seg_ext = jnp.concatenate([prev_ids, seg_ids])
    extended = jnp.concatenate([prev_rows, conv_seq]).astype(jnp.float32)
    conv_out, pull_conv = jax.vjp(
        lambda ext_in, kernel, offset: conv_mix(ext_in, seg_ext, kernel, offset),
        extended,
        kernel_f,
        offset_f,
    )
    (end_state, carry_gate), pull_state = jax.vjp(
        lambda mix_in, raw_in, bias_in, decay_in: state_local(
            mix_in, raw_in, bias_in, decay_in, seg_ids
        ),
        conv_out,
        raw_seq,
        step_bias,
        decay_log,
    )
    identity = (
        jnp.ones((H,), jnp.float32),
        jnp.zeros((H, P_SIZE, NS), jnp.float32),
        jnp.array(-1, jnp.int32),
        jnp.array(-1, jnp.int32),
    )
    prefix = entering(
        (carry_gate, end_state, seg_ids[0], seg_ids[local_rows - 1]), "fsdp", join_states, identity
    )
    prev_state = prefix[1]
    prev_last = prefix[3]
    mixer_out, pull_mixer = jax.vjp(
        lambda mix_in, raw_in, bias_in, decay_in, skip_in, state_in: mixer_output(
            mix_in, raw_in, bias_in, decay_in, skip_in, seg_ids, state_in, prev_last
        ),
        conv_out,
        raw_seq,
        step_bias,
        decay_log,
        skip_gain,
        prev_state,
    )
    saved_terms = (pull_conv, pull_state, pull_mixer, carry_gate, prev_state, prev_last, seg_ids)
    return (mixer_out, saved_terms)


def mixer_backward(saved_terms, grad_mixer):
    pull_conv, pull_state, pull_mixer, carry_gate, prev_state, prev_last, seg_ids = saved_terms
    local_rows = seg_ids.shape[0]
    halo_rows = KC - 1
    grad_mix_b, grad_raw_b, grad_bias_b, grad_decay_b, grad_skip, grad_prev = pull_mixer(grad_mixer)
    linked = (prev_last == seg_ids[0]).astype(jnp.float32)
    back_identity = (jnp.ones((H,), jnp.float32), jnp.zeros((H, P_SIZE, NS), jnp.float32))
    from_later = entering_2((carry_gate * linked, grad_prev), "fsdp", join_back, back_identity)[1]
    grad_gate = linked * jnp.sum(from_later * prev_state, axis=(1, 2))
    grad_mix_a, grad_raw_a, grad_bias_a, grad_decay_a = pull_state((from_later, grad_gate))
    grad_ext, grad_kernel, grad_offset = pull_conv(grad_mix_a + grad_mix_b)
    back_rows = from_behind(grad_ext[:halo_rows], "fsdp", -1)
    grad_conv_seq = jnp.concatenate(
        [grad_ext[halo_rows:local_rows], grad_ext[local_rows:] + back_rows]
    ).astype(jnp.bfloat16)
    return (
        grad_conv_seq,
        grad_raw_a + grad_raw_b,
        grad_kernel,
        grad_offset,
        grad_bias_a + grad_bias_b,
        grad_decay_a + grad_decay_b,
        grad_skip,
    )


def attend_forward(queries, key_value_rows, seg_ids, query_pos):
    local_rows = queries.shape[0]
    head_groups = QUERY_HEADS // KEY_VALUE_HEADS
    run_max = jnp.full((QUERY_HEADS, local_rows), NEGATIVE, jnp.float32)
    accumulated = jnp.zeros((local_rows, QUERY_HEADS, HEAD_WIDTH), jnp.float32)
    scores, allowed, segment_key_rows, segment_value_rows, grouped_heads = head_scores(
        queries,
        lax.all_gather(key_value_rows, "fsdp", axis=0, tiled=True),
        lax.all_gather(seg_ids, "fsdp", axis=0, tiled=True),
        query_pos,
        seg_ids,
    )
    segment_length = segment_key_rows.shape[0]
    new_max = jnp.maximum(run_max, jnp.max(scores, axis=-1))
    weight_set = jnp.where(allowed[None], jnp.exp(scores - new_max[:, :, None]), 0.0)
    factor = jnp.exp(run_max - new_max)
    new_sum = jnp.sum(weight_set, axis=-1)
    weight_set_reduced = weight_set.astype(jnp.bfloat16).reshape(
        KEY_VALUE_HEADS, head_groups, local_rows, segment_length
    )
    added = jnp.einsum(
        "gjqk,kgd->qgjd", weight_set_reduced, segment_value_rows, preferred_element_type=jnp.float32
    ).reshape(local_rows, QUERY_HEADS, HEAD_WIDTH)
    run_max, run_sum, accumulated = (new_max, new_sum, accumulated * factor.T[:, :, None] + added)
    attn_vals = accumulated / run_sum.T[:, :, None]
    log_sum = run_max + jnp.log(run_sum)
    return (attn_vals, log_sum)


def attend_backward(
    queries, key_value_rows, seg_ids, query_pos, log_sum, attn_vals, gradient_attention_values
):
    local_rows = queries.shape[0]
    head_groups = QUERY_HEADS // KEY_VALUE_HEADS
    score_scale = HEAD_WIDTH ** (-0.5)
    row_dot = jnp.sum(gradient_attention_values.astype(jnp.float32) * attn_vals, axis=-1).T
    gradient_attention_grouped = gradient_attention_values.reshape(
        local_rows, KEY_VALUE_HEADS, head_groups, HEAD_WIDTH
    )
    scores, allowed, segment_key_rows, segment_value_rows, grouped_heads = head_scores(
        queries,
        lax.all_gather(key_value_rows, "fsdp", axis=0, tiled=True),
        lax.all_gather(seg_ids, "fsdp", axis=0, tiled=True),
        query_pos,
        seg_ids,
    )
    segment_length = segment_key_rows.shape[0]
    weight_set = jnp.where(allowed[None], jnp.exp(scores - log_sum[:, :, None]), 0.0)
    weight_set_reduced = weight_set.astype(jnp.bfloat16).reshape(
        KEY_VALUE_HEADS, head_groups, local_rows, segment_length
    )
    gradient_value_rows = jnp.einsum(
        "gjqk,qgjd->kgd",
        weight_set_reduced,
        gradient_attention_grouped,
        preferred_element_type=jnp.float32,
    )
    grad_weights = jnp.einsum(
        "qgjd,kgd->gjqk",
        gradient_attention_grouped,
        segment_value_rows,
        preferred_element_type=jnp.float32,
    ).reshape(QUERY_HEADS, local_rows, segment_length)
    grad_scores = (
        (weight_set * (grad_weights - row_dot[:, :, None]))
        .astype(jnp.bfloat16)
        .reshape(KEY_VALUE_HEADS, head_groups, local_rows, segment_length)
    )
    grad_query = (
        jnp.einsum(
            "gjqk,kgd->qgjd", grad_scores, segment_key_rows, preferred_element_type=jnp.float32
        ).reshape(local_rows, QUERY_HEADS, HEAD_WIDTH)
        * score_scale
    )
    gradient_key_rows = (
        jnp.einsum("gjqk,qgjd->kgd", grad_scores, grouped_heads, preferred_element_type=jnp.float32)
        * score_scale
    )
    update = jnp.concatenate(
        [
            gradient_key_rows.reshape(segment_length, KEY_VALUE_HEADS * HEAD_WIDTH),
            gradient_value_rows.reshape(segment_length, KEY_VALUE_HEADS * HEAD_WIDTH),
        ],
        axis=1,
    )
    grad_query, grad_kv_all = (grad_query, update)
    grad_kv = lax.psum_scatter(
        grad_kv_all.astype(jnp.bfloat16), "fsdp", scatter_dimension=0, tiled=True
    )
    return (grad_query.astype(jnp.bfloat16).reshape(local_rows, QUERY_HEADS * HEAD_WIDTH), grad_kv)


def per_device(
    hidden_in,
    segment_ids,
    norm1_gain,
    w_gate_z,
    w_xbc,
    w_step,
    conv_weight,
    conv_bias,
    step_bias,
    decay_log,
    skip_gain,
    mixer_gain,
    w_mix_out,
    w_query,
    key_value_weight,
    w_attn_out,
    norm2_gain,
    w_gate_up,
    w_down,
    out_grad,
):
    local_sequence = hidden_in.shape[1]
    local_rows = hidden_in.shape[2]
    flat_rows = local_sequence * local_rows
    query_pos = lax.axis_index("fsdp") * local_rows + lax.iota(jnp.int32, local_rows)
    out_list = []
    grad_in_list = []
    shard_total = None
    bias_total = jnp.zeros((H,), jnp.float32)
    decay_total = jnp.zeros((H,), jnp.float32)
    skip_total = jnp.zeros((H,), jnp.float32)
    for micro_step in range(MB):
        fetched = (
            lax.all_gather(norm1_gain, ("dp", "fsdp"), axis=0, tiled=True),
            lax.all_gather(w_gate_z, ("dp", "fsdp"), axis=0, tiled=True),
            lax.all_gather(w_xbc, ("dp", "fsdp"), axis=0, tiled=True),
            lax.all_gather(w_step, ("dp", "fsdp"), axis=0, tiled=True),
            lax.all_gather(conv_weight, ("dp", "fsdp"), axis=1, tiled=True),
            lax.all_gather(conv_bias, ("dp", "fsdp"), axis=0, tiled=True),
            lax.all_gather(mixer_gain, ("dp", "fsdp"), axis=0, tiled=True),
            lax.all_gather(w_mix_out, ("dp", "fsdp"), axis=0, tiled=True),
            lax.all_gather(w_query, ("dp", "fsdp"), axis=0, tiled=True),
            lax.all_gather(key_value_weight, ("dp", "fsdp"), axis=0, tiled=True),
            lax.all_gather(w_attn_out, ("dp", "fsdp"), axis=0, tiled=True),
            lax.all_gather(norm2_gain, ("dp", "fsdp"), axis=0, tiled=True),
            lax.all_gather(w_gate_up, ("dp", "fsdp"), axis=0, tiled=True),
            lax.all_gather(w_down, ("dp", "fsdp"), axis=0, tiled=True),
        )
        (
            gain_one,
            gate_z_full,
            xbc_full,
            step_full,
            kernel_full,
            offset_full,
            mix_gain_full,
            mix_out_full,
            query_full,
            keyval_full,
            attn_out_full,
            gain_two,
            gate_up_full,
            down_full,
        ) = fetched
        kernel_f = kernel_full.astype(jnp.float32)
        offset_f = offset_full.astype(jnp.float32)
        tokens = hidden_in[micro_step].reshape(flat_rows, MODEL_WIDTH).astype(jnp.float32)
        seg_block = segment_ids[micro_step]
        normed, pull_norm_one = jax.vjp(rms_gain, tokens, gain_one.astype(jnp.float32))
        normed_low = normed.astype(jnp.bfloat16)
        gate_z = matmul(normed_low, gate_z_full)
        conv_in = (
            matmul(normed_low, xbc_full)
            .astype(jnp.bfloat16)
            .reshape(local_sequence, local_rows, DI + 2 * NS)
        )
        raw_step = matmul(normed_low, step_full).reshape(local_sequence, local_rows, H)
        queries = (
            matmul(normed_low, query_full)
            .astype(jnp.bfloat16)
            .reshape(local_sequence, local_rows, QUERY_HEADS * HEAD_WIDTH)
        )
        key_value_rows = (
            matmul(normed_low, keyval_full)
            .astype(jnp.bfloat16)
            .reshape(local_sequence, local_rows, 2 * KEY_VALUE_HEADS * HEAD_WIDTH)
        )
        seq_index = 0
        mixer_out, saved_terms = mixer_forward(
            conv_in[seq_index],
            seg_block[seq_index],
            raw_step[seq_index],
            kernel_f,
            offset_f,
            step_bias,
            decay_log,
            skip_gain,
        )
        saved_list = [saved_terms]
        attn_vals, log_sum = attend_forward(
            queries[seq_index], key_value_rows[seq_index], seg_block[seq_index], query_pos
        )
        attn_list = [attn_vals]
        lse_list = [log_sum]
        normed_mix, pull_gated = jax.vjp(
            gated_norm, mixer_out, gate_z, mix_gain_full.astype(jnp.float32)
        )
        normed_mix_low = normed_mix.astype(jnp.bfloat16)
        mamba_part = matmul(normed_mix_low, mix_out_full)
        attn_low = attn_list[0].astype(jnp.bfloat16).reshape(flat_rows, QUERY_HEADS * HEAD_WIDTH)
        attn_part = matmul(attn_low, attn_out_full)
        residual = tokens + mamba_part + attn_part
        normed_two, pull_norm_two = jax.vjp(rms_gain, residual, gain_two.astype(jnp.float32))
        normed_two_low = normed_two.astype(jnp.bfloat16)
        gate_up = matmul(normed_two_low, gate_up_full)
        activated, pull_swiglu = jax.vjp(swiglu, gate_up)
        act_low = activated.astype(jnp.bfloat16)
        block_out = residual + matmul(act_low, down_full)
        out_list.append(
            block_out.astype(jnp.bfloat16).reshape(local_sequence, local_rows, MODEL_WIDTH)
        )
        back_weights = (
            lax.all_gather(w_gate_z, ("dp", "fsdp"), axis=0, tiled=True),
            lax.all_gather(w_xbc, ("dp", "fsdp"), axis=0, tiled=True),
            lax.all_gather(w_step, ("dp", "fsdp"), axis=0, tiled=True),
            lax.all_gather(w_mix_out, ("dp", "fsdp"), axis=0, tiled=True),
            lax.all_gather(w_query, ("dp", "fsdp"), axis=0, tiled=True),
            lax.all_gather(key_value_weight, ("dp", "fsdp"), axis=0, tiled=True),
            lax.all_gather(w_attn_out, ("dp", "fsdp"), axis=0, tiled=True),
            lax.all_gather(w_gate_up, ("dp", "fsdp"), axis=0, tiled=True),
            lax.all_gather(w_down, ("dp", "fsdp"), axis=0, tiled=True),
        )
        (
            gate_z_bwd,
            xbc_bwd,
            step_bwd,
            mix_out_bwd,
            query_bwd,
            keyval_bwd,
            attn_out_bwd,
            gate_up_bwd,
            down_bwd,
        ) = back_weights
        grad_out = out_grad[micro_step].reshape(flat_rows, MODEL_WIDTH)
        grad_down = left_t(act_low, grad_out)
        (grad_gate_up,) = pull_swiglu(right_t(grad_out, down_bwd))
        grad_gate_up_low = grad_gate_up.astype(jnp.bfloat16)
        grad_gate_up_w = left_t(normed_two_low, grad_gate_up_low)
        grad_resid_norm, grad_gain_two = pull_norm_two(right_t(grad_gate_up_low, gate_up_bwd))
        grad_resid = grad_out.astype(jnp.float32) + grad_resid_norm
        grad_branch = grad_resid.astype(jnp.bfloat16)
        grad_attn_w = left_t(attn_low, grad_branch)
        grad_mix_out_w = left_t(normed_mix_low, grad_branch)
        gradient_attention_values = (
            right_t(grad_branch, attn_out_bwd)
            .astype(jnp.bfloat16)
            .reshape(local_sequence, local_rows, QUERY_HEADS, HEAD_WIDTH)
        )
        grad_mixer_all, grad_gate_z, grad_mix_gain = pull_gated(right_t(grad_branch, mix_out_bwd))
        grad_mixer_seq = grad_mixer_all.reshape(local_sequence, local_rows, DI)
        seq_index = 0
        grad_query_low, grad_kv = attend_backward(
            queries[seq_index],
            key_value_rows[seq_index],
            seg_block[seq_index],
            query_pos,
            lse_list[seq_index],
            attn_list[seq_index],
            gradient_attention_values[seq_index],
        )
        conv_seq, raw_seq, kernel_part, offset_part, bias_part, decay_part, skip_part = (
            mixer_backward(saved_list[seq_index], grad_mixer_seq[seq_index])
        )
        bias_total = bias_total + bias_part
        decay_total = decay_total + decay_part
        skip_total = skip_total + skip_part
        grad_raw_low = raw_seq.astype(jnp.bfloat16)
        grad_gate_z_low = grad_gate_z.astype(jnp.bfloat16)
        grad_normed = (
            right_t(grad_gate_z_low, gate_z_bwd)
            + right_t(conv_seq, xbc_bwd)
            + right_t(grad_raw_low, step_bwd)
            + right_t(grad_query_low, query_bwd)
            + right_t(grad_kv, keyval_bwd)
        )
        grad_tokens, grad_gain_one = pull_norm_one(grad_normed)
        grad_in_list.append(
            (grad_resid + grad_tokens).reshape(local_sequence, local_rows, MODEL_WIDTH)
        )
        grad_gate_z_w = left_t(normed_low, grad_gate_z_low)
        grad_xbc_w = left_t(normed_low, conv_seq)
        grad_step_w = left_t(normed_low, grad_raw_low)
        grad_query_w = left_t(normed_low, grad_query_low)
        grad_keyval_w = left_t(normed_low, grad_kv)
        owned_parts = (
            lax.psum_scatter(grad_gain_one, ("dp", "fsdp"), scatter_dimension=0, tiled=True),
            lax.psum_scatter(grad_gate_z_w, ("dp", "fsdp"), scatter_dimension=0, tiled=True),
            lax.psum_scatter(grad_xbc_w, ("dp", "fsdp"), scatter_dimension=0, tiled=True),
            lax.psum_scatter(grad_step_w, ("dp", "fsdp"), scatter_dimension=0, tiled=True),
            lax.psum_scatter(kernel_part, ("dp", "fsdp"), scatter_dimension=1, tiled=True),
            lax.psum_scatter(offset_part, ("dp", "fsdp"), scatter_dimension=0, tiled=True),
            lax.psum_scatter(grad_mix_gain, ("dp", "fsdp"), scatter_dimension=0, tiled=True),
            lax.psum_scatter(grad_mix_out_w, ("dp", "fsdp"), scatter_dimension=0, tiled=True),
            lax.psum_scatter(grad_query_w, ("dp", "fsdp"), scatter_dimension=0, tiled=True),
            lax.psum_scatter(grad_keyval_w, ("dp", "fsdp"), scatter_dimension=0, tiled=True),
            lax.psum_scatter(grad_attn_w, ("dp", "fsdp"), scatter_dimension=0, tiled=True),
            lax.psum_scatter(grad_gain_two, ("dp", "fsdp"), scatter_dimension=0, tiled=True),
            lax.psum_scatter(grad_gate_up_w, ("dp", "fsdp"), scatter_dimension=0, tiled=True),
            lax.psum_scatter(grad_down, ("dp", "fsdp"), scatter_dimension=0, tiled=True),
        )
        shard_total = (
            owned_parts if shard_total is None else jax.tree.map(jnp.add, shard_total, owned_parts)
        )
    head_sums = lax.psum((bias_total, decay_total, skip_total), ("dp", "fsdp"))
    hidden_out = jnp.stack(out_list)
    input_grad = jnp.stack(grad_in_list)
    return (
        hidden_out,
        input_grad,
        shard_total[0],
        shard_total[1],
        shard_total[2],
        shard_total[3],
        shard_total[4],
        shard_total[5],
        head_sums[0],
        head_sums[1],
        head_sums[2],
        shard_total[6],
        shard_total[7],
        shard_total[8],
        shard_total[9],
        shard_total[10],
        shard_total[11],
        shard_total[12],
        shard_total[13],
    )


def solution(mesh):
    placed = (
        P(None, "dp", "fsdp", None),
        P(None, "dp", "fsdp"),
        P(("dp", "fsdp")),
        P(("dp", "fsdp"), None),
        P(("dp", "fsdp"), None),
        P(("dp", "fsdp"), None),
        P(None, ("dp", "fsdp")),
        P(("dp", "fsdp")),
        P(),
        P(),
        P(),
        P(("dp", "fsdp")),
        P(("dp", "fsdp"), None),
        P(("dp", "fsdp"), None),
        P(("dp", "fsdp"), None),
        P(("dp", "fsdp"), None),
        P(("dp", "fsdp")),
        P(("dp", "fsdp"), None),
        P(("dp", "fsdp"), None),
        P(None, "dp", "fsdp", None),
    )
    return jax.shard_map(
        per_device,
        mesh=mesh,
        in_specs=placed,
        out_specs=(
            P(None, "dp", "fsdp", None),
            P(None, "dp", "fsdp", None),
            P(("dp", "fsdp")),
            P(("dp", "fsdp"), None),
            P(("dp", "fsdp"), None),
            P(("dp", "fsdp"), None),
            P(None, ("dp", "fsdp")),
            P(("dp", "fsdp")),
            P(),
            P(),
            P(),
            P(("dp", "fsdp")),
            P(("dp", "fsdp"), None),
            P(("dp", "fsdp"), None),
            P(("dp", "fsdp"), None),
            P(("dp", "fsdp"), None),
            P(("dp", "fsdp")),
            P(("dp", "fsdp"), None),
            P(("dp", "fsdp"), None),
        ),
        check_vma=False,
    )
```

profile of v0, /device:TPU:8, one launch (start us, length us, event | category | flops | bytes accessed | tf_op | source)
XLA Modules:
  0.0 1953.9 jit_solution(9883945907887958016)
XLA Ops:
  10.5 3.7 collective-permute-start.3
  19.7 40.0 %all-reduce.49 = (bf16[1024]{0:T(1024)(128)(2,1)S(1)}, bf16[1792]{0:T(1024)(128)(2,1)S(1)}, bf16[1536]{0:T(1024)(128)(2,1)S(1)}, bf16[1024]{0:T(1024)(128)(2,1)}) all-reduce(bf16[1024]{0:T(1024)(128)(2,1)S(1)} %dynamic-update-slice.1, bf16[1792]{0:T(1024)(128)(2,1)S(1)} %dynamic-update-slice, ...), channel_id=1, replica_groups=mesh['dp'=8,'fsdp'=4] {'dp','fsdp'}, use_global_device_ids=true, to_apply=%add.35 | all-reduce | flops 5376 | bytes 21504
  61.2 35.6 %all-gather.10 = bf16[32,56,4]{1,2,0:T(4,128)(2,1)S(1)} all-gather(bf16[1,56,4]{1,2,0:T(4,128)(2,1)} %bitcast.911), channel_id=1, replica_groups=mesh['dp'=8,'fsdp'=4] {'dp','fsdp'}, dimensions={0}, use_global_device_ids=true | all-gather | bytes 14784 | tf_op jit(solution)/shard_map/all_gather | solution.py:407
  97.1 37.5 %all-gather.11 = bf16[32,32,24]{1,2,0:T(8,128)(2,1)S(1)} all-gather(bf16[1,32,24]{1,2,0:T(8,128)(2,1)} %bitcast.904), channel_id=1, replica_groups=mesh['dp'=8,'fsdp'=4] {'dp','fsdp'}, dimensions={0}, use_global_device_ids=true | all-gather | bytes 50688 | tf_op jit(solution)/shard_map/all_gather | solution.py:406
  139.4 3.4 convolution_convert_fusion.1
  150.7 4.0 fusion.75
  171.4 3.6 fusion.124
  179.2 5.6 all-gather.3
  184.8 6.2 all-gather.7
  191.8 39.1 %all_gather.156 = bf16[1024,256]{1,0:T(8,128)(2,1)S(1)} all-gather(bf16[32,256]{1,0:T(8,128)(2,1)S(1)} %copy-done.213), channel_id=1, replica_groups=mesh['dp'=8,'fsdp'=4] {'dp','fsdp'}, dimensions={0}, use_global_device_ids=true | all-gather | bytes 540672 | tf_op jit(solution)/shard_map/all_gather | solution.py:412
  234.3 5.0 all-gather.13
  246.6 7.2 all_gather.169
  260.7 5.2 all-gather.12
  266.5 7.4 all_gather.157
  277.0 5.2 all-reduce.47
  307.4 6.3 fusion.28
  313.7 6.7 fusion.30
  333.4 9.0 fusion.82
  349.0 8.4 fusion.83
  360.7 37.2 %all-gather.15 = bf16[4,1,24]{2,1,0:T(2,128)(2,1)S(1)} all-gather(bf16[1,1,24]{2,1,0:T(2,128)(2,1)S(1)} %bitcast.907), channel_id=1, replica_groups=mesh['dp'=8,'fsdp'=4] {'fsdp'}, dimensions={0}, use_global_device_ids=true | all-gather | bytes 240 | tf_op jit(solution)/shard_map/all_gather | solution.py:57
  398.7 5.4 all-gather.14
  404.7 5.1 multiply_reduce_fusion.22
  410.4 4.4 fusion.114
  418.0 4.4 multiply_reduce_fusion.23
  425.8 41.4 %all-gather.38.cloned.1.call-done = bf16[1024,4096]{1,0:T(8,128)(2,1)} async-done(((bf16[32,4096]{1,0:T(8,128)(2,1)}), bf16[1024,4096]{1,0:T(8,128)(2,1)}) %all-gather.38.cloned.1.call-update) | async-done | bytes 8388624 | tf_op jit(solution)/shard_map/all_gather | solution.py:415
  467.2 8.4 fusion.351
  475.6 4.3 fusion.350
  479.9 50.7 %all-gather.40.cloned.1.call-done = bf16[2048,1024]{1,0:T(8,128)(2,1)} async-done(((bf16[64,1024]{1,0:T(8,128)(2,1)}), bf16[2048,1024]{1,0:T(8,128)(2,1)}) %all-gather.40.cloned.1.call-update) | async-done | bytes 4194320 | tf_op jit(solution)/shard_map/all_gather | solution.py:416
  530.7 6.7 fusion.241
  537.5 4.8 fusion.240
  545.0 6.1 multiply_reduce_fusion.25
  562.0 4.4 multiply_reduce_fusion.13
  566.5 7.5 multiply_reduce_fusion.15
  574.7 5.7 fusion.153
  580.4 5.1 fusion.3
  588.6 6.5 multiply_reduce_fusion.14
  606.9 12.4 fusion.39
  628.5 12.2 fusion.37
  644.9 5.6 fusion.1
  652.5 5.7 fusion.150
  661.5 4.0 while.61
  665.5 4.1 multiply_reduce_fusion.17
  670.3 3.7 while.60
  674.0 4.1 multiply_reduce_fusion.20
  710.8 3.7 convolution_add_fusion.2
  717.5 3.7 convolution_add_fusion.1
  724.1 4.7 convolution_add_fusion.4
  729.7 8.4 bitcast_add_fusion
  741.3 8.5 bitcast_add_fusion.1
  752.8 4.1 fusion.169
  777.1 3.8 multiply_reduce_fusion.7
  792.3 4.2 convolution_add_fusion.3
  797.7 10.7 fusion.233
  808.4 14.1 convolution_add_fusion
  824.2 3.9 fusion.146
  844.8 41.9 %all-reduce.48 = (f32[1024]{0:T(1024)S(1)}, f32[4,1792]{1,0:T(4,128)S(1)}, f32[1792]{0:T(1024)S(1)}, f32[24]{0:T(128)}, f32[24]{0:T(128)}, /*index=5*/f32[24]{0:T(128)}, f32[1536]{0:T(1024)S(1)}, f32[1024]{0:T(1024)S(1)}) all-reduce(f32[1024]{0:T(1024)S(1)} %add.619, ...), channel_id=28, replica_groups=mesh['dp'=8,'fsdp'=4] {'dp','fsdp'}, use_global_device_ids=true, to_apply=%region_57.59.clone | all-reduce | flops 12616 | bytes 100928
  895.8 45.4 %reduce-scatter.27.cloned.1.call-done = f32[32,256]{1,0:T(8,128)} async-done(((f32[1024,256]{1,0:T(8,128)}), f32[32,256]{1,0:T(8,128)}) %reduce-scatter.27.cloned.1.call-update) | async-done | bytes 32784 | tf_op jit(solution)/shard_map/reduce_scatter | solution.py:574
  941.2 135.4 %reduce-scatter.25.cloned.1.call-done = f32[32,512]{1,0:T(8,128)} async-done(((f32[1024,512]{1,0:T(8,128)}), f32[32,512]{1,0:T(8,128)}) %reduce-scatter.25.cloned.1.call-update) | async-done | bytes 65552 | tf_op jit(solution)/shard_map/reduce_scatter | solution.py:573
  1076.6 135.6 %reduce-scatter.29.cloned.1.call-done = f32[16,1024]{1,0:T(8,128)} async-done(((f32[512,1024]{1,0:T(8,128)}), f32[16,1024]{1,0:T(8,128)}) %reduce-scatter.29.cloned.1.call-update) | async-done | bytes 65552 | tf_op jit(solution)/shard_map/reduce_scatter | solution.py:575
  1212.2 135.1 %reduce-scatter.19.cloned.1.call-done = f32[32,1536]{1,0:T(8,128)} async-done(((f32[1024,1536]{1,0:T(8,128)}), f32[32,1536]{1,0:T(8,128)}) %reduce-scatter.19.cloned.1.call-update) | async-done | bytes 196624 | tf_op jit(solution)/shard_map/reduce_scatter | solution.py:566
  1347.3 120.7 %reduce-scatter.23.cloned.1.call-done = f32[48,1024]{1,0:T(8,128)} async-done(((f32[1536,1024]{1,0:T(8,128)}), f32[48,1024]{1,0:T(8,128)}) %reduce-scatter.23.cloned.1.call-update) | async-done | bytes 196624 | tf_op jit(solution)/shard_map/reduce_scatter | solution.py:572
  1468.0 131.7 %reduce-scatter.33.cloned.1.call-done = f32[64,1024]{1,0:T(8,128)} async-done(((f32[2048,1024]{1,0:T(8,128)}), f32[64,1024]{1,0:T(8,128)}) %reduce-scatter.33.cloned.1.call-update) | async-done | bytes 262160 | tf_op jit(solution)/shard_map/reduce_scatter | solution.py:578
  1599.7 145.7 %reduce-scatter.21.cloned.1.call-done = f32[32,1792]{1,0:T(8,128)} async-done(((f32[1024,1792]{1,0:T(8,128)}), f32[32,1792]{1,0:T(8,128)}) %reduce-scatter.21.cloned.1.call-update) | async-done | bytes 229392 | tf_op jit(solution)/shard_map/reduce_scatter | solution.py:567
  1745.5 201.4 %reduce-scatter.31.cloned.1.call-done = f32[32,4096]{1,0:T(8,128)} async-done(((f32[1024,4096]{1,0:T(8,128)}), f32[32,4096]{1,0:T(8,128)}) %reduce-scatter.31.cloned.1.call-update) | async-done | bytes 524304 | tf_op jit(solution)/shard_map/reduce_scatter | solution.py:577
  (889 shorter events, 276.9 us)
Async XLA Ops:
  7.2 127.7 %copy-start.4 = (bf16[2,1,256,1024]{3,2,1,0:T(8,128)(2,1)S(1)}, bf16[2,1,256,1024]{3,2,1,0:T(8,128)(2,1)}, u32[]{:S(2)}) copy-start(bf16[2,1,256,1024]{3,2,1,0:T(8,128)(2,1)} %param.29) | copy-start | bytes 3145732
  7.2 127.7 %copy-start.256 = (f32[24]{0:T(128)S(1)}, f32[24]{0:T(128)}, u32[]{:S(2)}) copy-start(f32[24]{0:T(128)} %param.38) | copy-start | bytes 292
  7.2 127.7 %copy-start.263 = (f32[24]{0:T(128)S(1)}, f32[24]{0:T(128)}, u32[]{:S(2)}) copy-start(f32[24]{0:T(128)} %param.37) | copy-start | bytes 292
  7.2 132.1 %all-gather.28.cloned.1.call-start = ((), (), s32[]{:S(2)}) async-start(), calls=%async_computation.11 | async-start | bytes 3784704 | tf_op jit(solution)/shard_map/all_gather | solution.py:405
  8.0 274.2 %all-gather.34.cloned.1.call-start = ((), (), s32[]{:S(2)}) async-start(), calls=%async_computation.14 | async-start | bytes 1081344 | tf_op jit(solution)/shard_map/all_gather | solution.py:411
  8.8 128.8 %collective-permute-start.1 = (s32[3]{0:T(128)S(1)}, s32[3]{0:T(128)S(1)}, u32[]{:S(2)}, u32[]{:S(2)}) collective-permute-start(s32[3]{0:T(128)S(1)} %get-tuple-element.539), channel_id=1, source_target_pairs={{0,1},{1,2},{2,3},{4,5},{5,6},{6,7},{8,9},{9,10},{10,11},{12,13},{... | collective-permute-start | bytes 44 | tf_op jit(solution)/shard_map/ppermute | solution.py:27
  10.5 127.9 %collective-permute-start.3 = (s32[3]{0:T(128)S(1)}, s32[3]{0:T(128)S(1)}, u32[]{:S(2)}, u32[]{:S(2)}) collective-permute-start(s32[3]{0:T(128)S(1)} %get-tuple-element.540), channel_id=1, source_target_pairs={{0,1},{1,2},{2,3},{4,5},{5,6},{6,7},{8,9},{9,10},{10,11},{12,13},{... | collective-permute-start | bytes 44 | tf_op jit(solution)/shard_map/ppermute | solution.py:27
  14.2 314.0 %all-gather.44.cloned.1.call-start = ((), (), s32[]{:S(2)}) async-start(), calls=%async_computation.21 | async-start | bytes 1966080 | tf_op jit(solution)/shard_map/all_gather | solution.py:33
  15.0 260.6 %copy-start.145 = (s32[1,1,256]{2,1,0:T(1,128)}, s32[1,1,256]{2,1,0:T(1,128)S(1)}, u32[]{:S(2)}) copy-start(s32[1,1,256]{2,1,0:T(1,128)S(1)} %get-tuple-element.541) | copy-start | bytes 3076
  15.0 260.6 %copy-start.147 = (s32[1,1,256]{2,1,0:T(1,128)}, s32[1,1,256]{2,1,0:T(1,128)S(1)}, u32[]{:S(2)}) copy-start(s32[1,1,256]{2,1,0:T(1,128)S(1)} %get-tuple-element.542) | copy-start | bytes 3076
  61.2 73.7 %copy-start.222 = (f32[256]{0:T(256)}, f32[256]{0:T(256)S(1)}, u32[]{:S(2)}) copy-start(f32[256]{0:T(256)S(1)} %get-tuple-element.373) | copy-start | bytes 3076
  61.2 78.0 %copy-start.224 = (f32[256]{0:T(256)}, f32[256]{0:T(256)S(1)}, u32[]{:S(2)}) copy-start(f32[256]{0:T(256)S(1)} %get-tuple-element.374) | copy-start | bytes 3076
  61.2 170.2 %copy-start.156 = (f32[256]{0:T(256)}, f32[256]{0:T(256)S(1)}, u32[]{:S(2)}) copy-start(f32[256]{0:T(256)S(1)} %fusion.316) | copy-start | bytes 3076
  97.0 53.6 %copy-start.133 = (f32[1792]{0:T(1024)}, f32[1792]{0:T(1024)S(1)}, u32[]{:S(2)}) copy-start(f32[1792]{0:T(1024)S(1)} %get-tuple-element.375) | copy-start | bytes 21508
  97.0 53.6 %copy-start.135 = (f32[1792]{0:T(1024)}, f32[1792]{0:T(1024)S(1)}, u32[]{:S(2)}) copy-start(f32[1792]{0:T(1024)S(1)} %get-tuple-element.376) | copy-start | bytes 21508
  97.0 53.6 %copy-start.137 = (f32[1792]{0:T(1024)}, f32[1792]{0:T(1024)S(1)}, u32[]{:S(2)}) copy-start(f32[1792]{0:T(1024)S(1)} %get-tuple-element.377) | copy-start | bytes 21508
  97.1 53.6 %copy-start.139 = (f32[1792]{0:T(1024)}, f32[1792]{0:T(1024)S(1)}, u32[]{:S(2)}) copy-start(f32[1792]{0:T(1024)S(1)} %get-tuple-element.378) | copy-start | bytes 21508
  97.1 133.9 %copy-start.174 = (f32[256]{0:T(256)}, f32[256]{0:T(256)S(1)}, u32[]{:S(2)}) copy-start(f32[256]{0:T(256)S(1)} %fusion.319) | copy-start | bytes 3076
  134.9 28.1 %copy-start.98 = (bf16[1024,24]{0,1:T(8,128)(2,1)}, bf16[1024,24]{0,1:T(8,128)(2,1)S(1)}, u32[]{:S(2)}) copy-start(bf16[1024,24]{0,1:T(8,128)(2,1)S(1)} %reshape.995) | copy-start | bytes 147460
  134.9 28.4 %copy-start.226 = (f32[24]{0:T(128)}, f32[24]{0:T(128)S(1)}, u32[]{:S(2)}) copy-start(f32[24]{0:T(128)S(1)} %exp.106) | copy-start | bytes 292
  137.4 96.7 %copy-start.126 = (f32[256,24]{0,1:T(8,128)}, f32[256,24]{0,1:T(8,128)S(1)}, u32[]{:S(2)}) copy-start(f32[256,24]{0,1:T(8,128)S(1)} %get-tuple-element.522) | copy-start | bytes 73732
  138.4 27.2 %copy-start.209 = (f32[256]{0:T(256)}, f32[256]{0:T(256)S(1)}, u32[]{:S(2)}) copy-start(f32[256]{0:T(256)S(1)} %get-tuple-element.549) | copy-start | bytes 3076
  139.3 526.2 %copy-start.100 = (f32[256,24]{0,1:T(8,128)}, f32[256,24]{0,1:T(8,128)S(1)}, u32[]{:S(2)}) copy-start(f32[256,24]{0,1:T(8,128)S(1)} %multiply_multiply_fusion.8) | copy-start | bytes 73732
  142.8 6.8 collective-permute-start
  146.3 4.1 collective-permute-start.2
  159.1 174.2 %copy-start.18 = (f32[256,1536]{0,1:T(8,128)}, f32[256,1536]{0,1:T(8,128)S(1)}, u32[]{:S(2)}) copy-start(f32[256,1536]{0,1:T(8,128)S(1)} %copy.259) | copy-start | bytes 4718596
  162.4 183.1 %all-gather.42.cloned.1.call-start = ((), (), s32[]{:S(2)}) async-start(), calls=%async_computation.20 | async-start | bytes 1966080 | tf_op jit(solution)/shard_map/all_gather | solution.py:33
  165.4 95.1 %copy-start.129 = (f32[256,24]{0,1:T(8,128)}, f32[256,24]{0,1:T(8,128)S(1)}, u32[]{:S(2)}) copy-start(f32[256,24]{0,1:T(8,128)S(1)} %get-tuple-element.518) | copy-start | bytes 73732
  165.7 508.3 %copy-start.102 = (f32[256,24]{0,1:T(8,128)}, f32[256,24]{0,1:T(8,128)S(1)}, u32[]{:S(2)}) copy-start(f32[256,24]{0,1:T(8,128)S(1)} %multiply_multiply_fusion.9) | copy-start | bytes 73732
  171.4 20.4 %copy-start.213 = (bf16[32,256]{1,0:T(8,128)(2,1)S(1)}, bf16[32,256]{1,0:T(8,128)(2,1)}, u32[]{:S(2)}) copy-start(bf16[32,256]{1,0:T(8,128)(2,1)} %param.43) | copy-start | bytes 49156
  175.0 229.7 %all-gather.30.cloned.1.call-start = ((), (), s32[]{:S(2)}) async-start(), calls=%async_computation.12 | async-start | bytes 3244032 | tf_op jit(solution)/shard_map/all_gather | solution.py:404
  175.6 234.3 %all-gather.32.cloned.1.call-start = ((), (), s32[]{:S(2)}) async-start(), calls=%async_computation.13 | async-start | bytes 3244032 | tf_op jit(solution)/shard_map/all_gather | solution.py:410
  176.2 238.7 %all-gather.36.cloned.1.call-start = ((), (), s32[]{:S(2)}) async-start(), calls=%async_computation.15 | async-start | bytes 1081344 | tf_op jit(solution)/shard_map/all_gather | solution.py:413
  176.9 290.3 %all-gather.38.cloned.1.call-start = ((), (), s32[]{:S(2)}) async-start(), calls=%async_computation.16 | async-start | bytes 8650752 | tf_op jit(solution)/shard_map/all_gather | solution.py:415
  177.7 353.0 %all-gather.40.cloned.1.call-start = ((), (), s32[]{:S(2)}) async-start(), calls=%async_computation.17 | async-start | bytes 4325376 | tf_op jit(solution)/shard_map/all_gather | solution.py:416
  178.4 480.7 %reduce-scatter.15.cloned.1.call-start = ((), (), s32[]{:S(2)}) async-start(), calls=%async_computation.18 | async-start | bytes 655360 | tf_op jit(solution)/shard_map/reduce_scatter | solution.py:363
  255.5 30.9 %copy-start.69 = (bf16[1024,128]{0,1:T(8,128)(2,1)}, bf16[1024,128]{0,1:T(8,128)(2,1)S(1)}, u32[]{:S(2)}) copy-start(bf16[1024,128]{0,1:T(8,128)(2,1)S(1)} %copy.263) | copy-start | bytes 786436
  256.2 295.0 %copy-start.86 = (f32[1024]{0:T(1024)}, f32[1024]{0:T(1024)S(1)}, u32[]{:S(2)}) copy-start(f32[1024]{0:T(1024)S(1)} %convert_element_type.406) | copy-start | bytes 12292
  277.0 30.4 %copy-start.55 = (pred[256,1024]{0,1:T(8,128)(4,1)}, pred[256,1024]{0,1:T(8,128)(4,1)S(1)}, u32[]{:S(2)}) copy-start(pred[256,1024]{0,1:T(8,128)(4,1)S(1)} %get-tuple-element.548) | copy-start | bytes 786436
  277.0 36.7 %copy-start.57 = (pred[256,1024]{0,1:T(8,128)(4,1)}, pred[256,1024]{0,1:T(8,128)(4,1)S(1)}, u32[]{:S(2)}) copy-start(pred[256,1024]{0,1:T(8,128)(4,1)S(1)} %get-tuple-element.547) | copy-start | bytes 786436
  294.2 26.3 %copy-start.143 = (f32[8,256]{1,0:T(8,128)}, f32[8,256]{1,0:T(8,128)S(1)}, u32[]{:S(2)}) copy-start(f32[8,256]{1,0:T(8,128)S(1)} %reduce_sum.553) | copy-start | bytes 24580
  357.4 41.1 %copy-start.130 = (f32[256,24]{0,1:T(8,128)S(1)}, f32[256,24]{0,1:T(8,128)}, u32[]{:S(2)}) copy-start(f32[256,24]{0,1:T(8,128)} %copy-done.129) | copy-start | bytes 73732
  357.4 47.3 %copy-start.175 = (f32[256]{0:T(256)S(1)}, f32[256]{0:T(256)}, u32[]{:S(2)}) copy-start(f32[256]{0:T(256)} %copy-done.174) | copy-start | bytes 3076
  418.0 133.2 %copy-start.162 = (f32[256]{0:T(256)}, f32[256]{0:T(256)S(1)}, u32[]{:S(2)}) copy-start(f32[256]{0:T(256)S(1)} %fusion.321) | copy-start | bytes 3076
  425.8 125.4 %copy-start.160 = (f32[256]{0:T(256)}, f32[256]{0:T(256)S(1)}, u32[]{:S(2)}) copy-start(f32[256]{0:T(256)S(1)} %fusion.318) | copy-start | bytes 3076
  588.5 72.9 %all-gather.48.cloned.1.call-start = ((), (), s32[]{:S(2)}) async-start(), calls=%async_computation.23 | async-start | bytes 1966080 | tf_op jit(solution)/shard_map/all_gather | solution.py:57
  606.7 63.1 %all-gather.46.cloned.1.call-start = ((), (), s32[]{:S(2)}) async-start(), calls=%async_computation.22 | async-start | bytes 1966080 | tf_op jit(solution)/shard_map/all_gather | solution.py:57
  628.5 16.4 copy-start.56
  628.5 16.4 copy-start.115
  640.8 53.3 %reduce-scatter.17.cloned.1.call-start = ((), (), s32[]{:S(2)}) async-start(), calls=%async_computation.19 | async-start | bytes 655360 | tf_op jit(solution)/shard_map/reduce_scatter | solution.py:363
  659.0 235.4 %reduce-scatter.35.cloned.1.call-start = ((), (), s32[]{:S(2)}) async-start(), calls=%async_computation.32 | async-start | bytes 540672
  694.0 247.2 %reduce-scatter.27.cloned.1.call-start = ((), (), s32[]{:S(2)}) async-start(), calls=%async_computation.28 | async-start | bytes 1081344 | tf_op jit(solution)/shard_map/reduce_scatter | solution.py:574
  697.0 379.6 %reduce-scatter.25.cloned.1.call-start = ((), (), s32[]{:S(2)}) async-start(), calls=%async_computation.27 | async-start | bytes 2162688 | tf_op jit(solution)/shard_map/reduce_scatter | solution.py:573
  704.3 507.9 %reduce-scatter.29.cloned.1.call-start = ((), (), s32[]{:S(2)}) async-start(), calls=%async_computation.29 | async-start | bytes 2162688 | tf_op jit(solution)/shard_map/reduce_scatter | solution.py:575
  707.8 639.5 %reduce-scatter.19.cloned.1.call-start = ((), (), s32[]{:S(2)}) async-start(), calls=%async_computation.24 | async-start | bytes 6488064 | tf_op jit(solution)/shard_map/reduce_scatter | solution.py:566
  714.6 753.4 %reduce-scatter.23.cloned.1.call-start = ((), (), s32[]{:S(2)}) async-start(), calls=%async_computation.26 | async-start | bytes 6488064 | tf_op jit(solution)/shard_map/reduce_scatter | solution.py:572
  721.2 878.5 %reduce-scatter.33.cloned.1.call-start = ((), (), s32[]{:S(2)}) async-start(), calls=%async_computation.31 | async-start | bytes 8650752 | tf_op jit(solution)/shard_map/reduce_scatter | solution.py:578
  728.8 1016.7 %reduce-scatter.21.cloned.1.call-start = ((), (), s32[]{:S(2)}) async-start(), calls=%async_computation.25 | async-start | bytes 7569408 | tf_op jit(solution)/shard_map/reduce_scatter | solution.py:567
  785.1 4.3 collective-permute-start.5
  787.9 4.4 collective-permute-start.4
  796.5 1150.4 %reduce-scatter.31.cloned.1.call-start = ((), (), s32[]{:S(2)}) async-start(), calls=%async_computation.30 | async-start | bytes 17301504 | tf_op jit(solution)/shard_map/reduce_scatter | solution.py:577
  842.5 47.2 %copy-start.223 = (f32[256]{0:T(256)S(1)}, f32[256]{0:T(256)}, u32[]{:S(2)}) copy-start(f32[256]{0:T(256)} %copy-done.222) | copy-start | bytes 3076
  842.5 47.2 %copy-start.225 = (f32[256]{0:T(256)S(1)}, f32[256]{0:T(256)}, u32[]{:S(2)}) copy-start(f32[256]{0:T(256)} %copy-done.224) | copy-start | bytes 3076
  842.5 47.2 %copy-start.218 = (f32[256]{0:T(256)S(1)}, f32[256]{0:T(256)}, u32[]{:S(2)}) copy-start(f32[256]{0:T(256)} %copy-done.217) | copy-start | bytes 3076
  (235 other events, 1000.4 us)
Sparse Core Ops, SparseCore 0:
  10.9 61.6 all-gather.27
  75.5 52.0 all-gather.33
  162.5 24.3 all-gather.43
  188.3 21.2 all-gather.41
  212.3 59.0 all-gather.29
  274.1 57.0 all-gather.31
  334.1 52.7 all-gather.35
  389.8 77.4 all-gather.37
  470.1 60.5 all-gather.39
  588.7 20.2 reduce-scatter.14
  610.6 19.6 all-gather.47
  640.9 18.2 all-gather.45
  662.5 21.5 reduce-scatter.16
  694.1 113.2 reduce-scatter.34
  810.2 130.9 reduce-scatter.26
  943.9 132.6 reduce-scatter.24
  1079.4 132.7 reduce-scatter.28
  1218.3 129.0 reduce-scatter.18
  1354.5 113.5 reduce-scatter.22
  1470.8 128.9 reduce-scatter.32
  1602.6 142.7 reduce-scatter.20
  1748.3 198.5 reduce-scatter.30
where the time goes:
time: 1970 us; the launch traced here: 1950 us
  waiting for transfers between devices  1150 us (58%)
  matrix products  311 us (16%)
  blocking collectives  279 us (14%)
  local copies, waits for them, and re-layouts  94.6 us (5%)
  other arithmetic  83.4 us (4%)
  between operations  22 us (1%)
    reduce_scatter x1, waiting for transfers between devices, per_device(): lax.psum_scatter(grad_gate_up_w, ('dp', 'fsdp'), scatter_dimension=0, til...  201 us
    reduce_scatter x1, waiting for transfers between devices, per_device(): lax.psum_scatter(grad_xbc_w, ('dp', 'fsdp'), scatter_dimension=0, tiled=T...  146 us
    reduce_scatter x1, waiting for transfers between devices, per_device(): lax.psum_scatter(grad_attn_w, ('dp', 'fsdp'), scatter_dimension=0, tiled=...  136 us
    reduce_scatter x1, waiting for transfers between devices, per_device(): lax.psum_scatter(grad_query_w, ('dp', 'fsdp'), scatter_dimension=0, tiled...  135 us
    reduce_scatter x1, waiting for transfers between devices, per_device(): lax.psum_scatter(grad_gate_z_w, ('dp', 'fsdp'), scatter_dimension=0, tile...  135 us
    reduce_scatter x1, waiting for transfers between devices, per_device(): lax.psum_scatter(grad_down, ('dp', 'fsdp'), scatter_dimension=0, tiled=True)  132 us
    reduce_scatter x1, waiting for transfers between devices, per_device(): lax.psum_scatter(grad_mix_out_w, ('dp', 'fsdp'), scatter_dimension=0, til...  121 us
    unnamed x2, blocking collectives  82 us
  transfers between devices with their start and end apart: 28, of which 11 were waited for; matrix products, arithmetic and copies ran while one was open for 21% of the time, Pallas kernels for 0%

commit v1 on v0

--- a/solution.py
+++ b/solution.py
@@ -1,6 +1,8 @@
 import jax
 import jax.numpy as jnp
 from jax import lax
+from jax.experimental import pallas as pl
+from jax.experimental.pallas import tpu as pltpu
 from jax.sharding import PartitionSpec as P
 
 MODEL_WIDTH = 1024
@@ -366,6 +368,177 @@
     return (grad_query.astype(jnp.bfloat16).reshape(local_rows, QUERY_HEADS * HEAD_WIDTH), grad_kv)
 
 
+BOTH = ("dp", "fsdp")
+
+
+def exchange(block, bit):
+    count = lax.axis_size(BOTH)
+    return lax.ppermute(block, BOTH, [(i, i ^ (1 << bit)) for i in range(count)])
+
+
+def bit_count():
+    return lax.axis_size(BOTH).bit_length() - 1
+
+
+def place_of():
+    return lax.axis_index(BOTH)
+
+
+def gather_pieces(packed):
+    grown = packed[None]
+    offsets = [0]
+    for bit in range(bit_count() - 1, 2, -1):
+        grown = jnp.concatenate([grown, exchange(grown, bit)], 0)
+        offsets = offsets + [o ^ (1 << bit) for o in offsets]
+    halves = []
+    for half, (first, second) in enumerate(((2, 1), (1, 2))):
+        own = grown[:, half]
+        eight = jnp.concatenate([own, exchange(own, first)], 0)
+        near = offsets + [o ^ (1 << first) for o in offsets]
+        far_block = exchange(eight, second)
+        far = [o ^ (1 << second) for o in near]
+        halves.append(
+            [
+                (eight, near),
+                (far_block, far),
+                (exchange(eight, 0), [o ^ 1 for o in near]),
+                (exchange(far_block, 0), [o ^ 1 for o in far]),
+            ]
+        )
+    return halves
+
+
+def assemble(halves, outs, moves):
+    flat, meta = [], []
+    for half, pieces in enumerate(halves):
+        for piece, offsets in pieces:
+            flat.append(piece)
+            meta.append((half, offsets))
+    jobs = []
+    for at, (half, offsets) in enumerate(meta):
+        for j, offset in enumerate(offsets):
+            for move in moves:
+                if move[0] == half:
+                    jobs.append((at, j, offset, move))
+    jobs.sort(key=lambda job: job[3][3])
+    n_in, n_out = len(flat), len(outs)
+
+    def kernel(place_ref, *refs):
+        ins, results = refs[:n_in], refs[n_in : n_in + n_out]
+        held, sems, out_sems = refs[n_in + n_out : -2], refs[-2], refs[-1]
+        place = place_ref[0]
+        copies = [[] for _ in outs]
+        for number, (at, j, offset, (_, r0, rows, c0, columns, out, row, column)) in enumerate(jobs):
+            copy = pltpu.make_async_copy(
+                ins[at].at[j, pl.ds(r0, rows), pl.ds(c0, columns)],
+                held[out].at[place ^ offset, pl.ds(row, rows), pl.ds(column, columns)],
+                sems.at[number],
+            )
+            copy.start()
+            copies[out].append(copy)
+        back = []
+        for out in range(n_out):
+            for copy in copies[out]:
+                copy.wait()
+            copy = pltpu.make_async_copy(held[out], results[out], out_sems.at[out])
+            copy.start()
+            back.append(copy)
+        for copy in back:
+            copy.wait()
+
+    return pl.pallas_call(
+        kernel,
+        out_shape=[jax.ShapeDtypeStruct(s, jnp.bfloat16) for s in outs],
+        in_specs=[pl.BlockSpec(memory_space=pltpu.SMEM)]
+        + [pl.BlockSpec(memory_space=pl.ANY)] * n_in,
+        out_specs=[pl.BlockSpec(memory_space=pl.ANY)] * n_out,
+        scratch_shapes=[pltpu.VMEM(s, jnp.bfloat16) for s in outs]
+        + [pltpu.SemaphoreType.DMA((len(jobs),)), pltpu.SemaphoreType.DMA((n_out,))],
+        compiler_params=pltpu.CompilerParams(vmem_limit_bytes=24 * 2**20),
+        name="assemble",
+    )(place_of().reshape(1).astype(jnp.int32), *flat)
+
+
+def halve(block, axis, bit, last=False):
+    own_bit = (place_of() >> bit) & 1
+    mine = lax.dynamic_index_in_dim(block, own_bit, axis, False)
+    other = lax.dynamic_index_in_dim(block, 1 - own_bit, axis, False)
+    summed = mine.astype(jnp.float32) + exchange(other, bit).astype(jnp.float32)
+    return summed if last else summed.astype(jnp.bfloat16)
+
+
+def scatter_sum(first_half, second_half):
+    bits = bit_count()
+    count = 1 << bits
+    halves = []
+    for block, first in ((first_half, 2), (second_half, 1)):
+        rows, columns = block.shape[0] // count, block.shape[1]
+        block = block.astype(jnp.bfloat16).reshape((2,) * bits + (rows, columns))
+        block = halve(block, bits - 1, 0)
+        if first == 2:
+            block = halve(halve(block, bits - 3, 2), bits - 3, 1)
+        else:
+            block = halve(halve(block, bits - 2, 1), bits - 3, 2)
+        halves.append(block)
+    block = jnp.stack(halves)
+    for bit in range(3, bits):
+        block = halve(block, bits - bit, bit, last=bit == bits - 1)
+    return block
+
+
+def gather_weights(w_gate_z, w_xbc, w_step, w_query, key_value_weight, w_mix_out, w_attn_out, w_gate_up, w_down):
+    count = lax.axis_size(BOTH)
+    r = w_xbc.shape[0]
+    rm, ra, rd = w_mix_out.shape[0], w_attn_out.shape[0], w_down.shape[0]
+    step_pad = jnp.pad(w_step, ((0, 0), (0, 128 - H)))
+    one = jnp.concatenate([w_xbc, step_pad, w_query, key_value_weight], 1)
+    n1 = one.shape[1]
+    pad1 = -n1 % 256
+    one = jnp.pad(one, ((0, 0), (0, pad1)))
+    h1 = (n1 + pad1) // 2
+    one = jnp.stack([one[:, :h1], one[:, h1:]])
+    (first_full,) = assemble(
+        gather_pieces(one),
+        [(count, r, n1 + pad1)],
+        [(0, 0, r, 0, h1, 0, 0, 0), (1, 0, r, 0, h1, 0, 0, h1)],
+    )
+    z2 = jnp.stack([w_gate_z[:, : DI // 2], w_gate_z[:, DI // 2 :]])
+    (z_full,) = assemble(
+        gather_pieces(z2),
+        [(count, r, DI)],
+        [(0, 0, r, 0, DI // 2, 0, 0, 0), (1, 0, r, 0, DI // 2, 0, 0, DI // 2)],
+    )
+    hw = MODEL_WIDTH // 2
+    out2 = jnp.concatenate([w_mix_out, w_attn_out], 0)
+    out2 = jnp.stack([out2[:, :hw], out2[:, hw:]])
+    mix_full, attn_full = assemble(
+        gather_pieces(out2),
+        [(count, rm, MODEL_WIDTH), (count, ra, MODEL_WIDTH)],
+        [
+            (0, 0, rm, 0, hw, 0, 0, 0),
+            (1, 0, rm, 0, hw, 0, 0, hw),
+            (0, rm, ra, 0, hw, 1, 0, 0),
+            (1, rm, ra, 0, hw, 1, 0, hw),
+        ],
+    )
+    gu2 = jnp.stack([w_gate_up[:, :FF], w_gate_up[:, FF:]])
+    (gate_up_full,) = assemble(
+        gather_pieces(gu2),
+        [(count, r, 2 * FF)],
+        [(0, 0, r, 0, FF, 0, 0, 0), (1, 0, r, 0, FF, 0, 0, FF)],
+    )
+    d2 = jnp.stack([w_down[:, :hw], w_down[:, hw:]])
+    (down_full,) = assemble(
+        gather_pieces(d2),
+        [(count, rd, MODEL_WIDTH)],
+        [(0, 0, rd, 0, hw, 0, 0, 0), (1, 0, rd, 0, hw, 0, 0, hw)],
+    )
+    return tuple(
+        a.reshape(-1, a.shape[2])
+        for a in (first_full, z_full, mix_full, attn_full, gate_up_full, down_full)
+    )
+
+
 def per_device(
     hidden_in,
     segment_ids,
@@ -388,221 +561,151 @@
     w_down,
     out_grad,
 ):
-    local_sequence = hidden_in.shape[1]
     local_rows = hidden_in.shape[2]
-    flat_rows = local_sequence * local_rows
+    seqs = hidden_in.shape[0] * hidden_in.shape[1]
+    flat_rows = seqs * local_rows
+    conv_width = DI + 2 * NS
+    query_width = QUERY_HEADS * HEAD_WIDTH
+    kv_width = 2 * KEY_VALUE_HEADS * HEAD_WIDTH
     query_pos = lax.axis_index("fsdp") * local_rows + lax.iota(jnp.int32, local_rows)
-    out_list = []
-    grad_in_list = []
-    shard_total = None
-    bias_total = jnp.zeros((H,), jnp.float32)
-    decay_total = jnp.zeros((H,), jnp.float32)
-    skip_total = jnp.zeros((H,), jnp.float32)
-    for micro_step in range(MB):
-        fetched = (
-            lax.all_gather(norm1_gain, ("dp", "fsdp"), axis=0, tiled=True),
-            lax.all_gather(w_gate_z, ("dp", "fsdp"), axis=0, tiled=True),
-            lax.all_gather(w_xbc, ("dp", "fsdp"), axis=0, tiled=True),
-            lax.all_gather(w_step, ("dp", "fsdp"), axis=0, tiled=True),
-            lax.all_gather(conv_weight, ("dp", "fsdp"), axis=1, tiled=True),
-            lax.all_gather(conv_bias, ("dp", "fsdp"), axis=0, tiled=True),
-            lax.all_gather(mixer_gain, ("dp", "fsdp"), axis=0, tiled=True),
-            lax.all_gather(w_mix_out, ("dp", "fsdp"), axis=0, tiled=True),
-            lax.all_gather(w_query, ("dp", "fsdp"), axis=0, tiled=True),
-            lax.all_gather(key_value_weight, ("dp", "fsdp"), axis=0, tiled=True),
-            lax.all_gather(w_attn_out, ("dp", "fsdp"), axis=0, tiled=True),
-            lax.all_gather(norm2_gain, ("dp", "fsdp"), axis=0, tiled=True),
-            lax.all_gather(w_gate_up, ("dp", "fsdp"), axis=0, tiled=True),
-            lax.all_gather(w_down, ("dp", "fsdp"), axis=0, tiled=True),
+    pieces = [norm1_gain, norm2_gain, mixer_gain, conv_bias, conv_weight.reshape(-1)]
+    sizes = [p.shape[0] for p in pieces]
+    small = jnp.concatenate(pieces)
+    small_pad = -small.shape[0] % 128
+    small = jnp.pad(small, (0, small_pad))[None]
+    small_all = lax.all_gather(small, BOTH, axis=0, tiled=True).astype(jnp.float32)
+    vectors = []
+    at = 0
+    for size in sizes:
+        vectors.append(small_all[:, at : at + size])
+        at += size
+    gain_one, gain_two, mix_gain_full, offset_f = (v.reshape(-1) for v in vectors[:4])
+    kernel_f = vectors[4].reshape(vectors[4].shape[0], KC, -1).transpose(1, 0, 2).reshape(KC, -1)
+    first_full, z_full, mix_out_full, attn_out_full, gate_up_full, down_full = gather_weights(
+        w_gate_z, w_xbc, w_step, w_query, key_value_weight, w_mix_out, w_attn_out, w_gate_up, w_down
+    )
+    tokens = hidden_in.reshape(flat_rows, MODEL_WIDTH).astype(jnp.float32)
+    seg_block = segment_ids.reshape(seqs, local_rows)
+    normed, pull_norm_one = jax.vjp(rms_gain, tokens, gain_one)
+    normed_low = normed.astype(jnp.bfloat16)
+    first_out = matmul(normed_low, first_full)
+    conv_in = first_out[:, :conv_width].astype(jnp.bfloat16).reshape(seqs, local_rows, conv_width)
+    raw_step = first_out[:, conv_width : conv_width + H].reshape(seqs, local_rows, H)
+    q0 = conv_width + 128
+    queries = first_out[:, q0 : q0 + query_width].astype(jnp.bfloat16)
+    queries = queries.reshape(seqs, local_rows, query_width)
+    k0 = q0 + query_width
+    key_value_rows = first_out[:, k0 : k0 + kv_width].astype(jnp.bfloat16)
+    key_value_rows = key_value_rows.reshape(seqs, local_rows, kv_width)
+    gate_z = matmul(normed_low, z_full)
+    mixers, saved, attns, log_sums = [], [], [], []
+    for s in range(seqs):
+        mixer_out, saved_terms = mixer_forward(
+            conv_in[s], seg_block[s], raw_step[s], kernel_f, offset_f, step_bias, decay_log, skip_gain
         )
-        (
-            gain_one,
-            gate_z_full,
-            xbc_full,
-            step_full,
-            kernel_full,
-            offset_full,
-            mix_gain_full,
-            mix_out_full,
-            query_full,
-            keyval_full,
-            attn_out_full,
-            gain_two,
-            gate_up_full,
-            down_full,
-        ) = fetched
-        kernel_f = kernel_full.astype(jnp.float32)
-        offset_f = offset_full.astype(jnp.float32)
-        tokens = hidden_in[micro_step].reshape(flat_rows, MODEL_WIDTH).astype(jnp.float32)
-        seg_block = segment_ids[micro_step]
-        normed, pull_norm_one = jax.vjp(rms_gain, tokens, gain_one.astype(jnp.float32))
-        normed_low = normed.astype(jnp.bfloat16)
-        gate_z = matmul(normed_low, gate_z_full)
-        conv_in = (
-            matmul(normed_low, xbc_full)
-            .astype(jnp.bfloat16)
-            .reshape(local_sequence, local_rows, DI + 2 * NS)
+        mixers.append(mixer_out)
+        saved.append(saved_terms)
+        attn_vals, log_sum = attend_forward(queries[s], key_value_rows[s], seg_block[s], query_pos)
+        attns.append(attn_vals)
+        log_sums.append(log_sum)
+    mixer_out = jnp.concatenate(mixers)
+    normed_mix, pull_gated = jax.vjp(gated_norm, mixer_out, gate_z, mix_gain_full)
+    normed_mix_low = normed_mix.astype(jnp.bfloat16)
+    attn_low = jnp.concatenate(attns).astype(jnp.bfloat16).reshape(flat_rows, query_width)
+    residual = tokens + (matmul(normed_mix_low, mix_out_full) + matmul(attn_low, attn_out_full))
+    normed_two, pull_norm_two = jax.vjp(rms_gain, residual, gain_two)
+    normed_two_low = normed_two.astype(jnp.bfloat16)
+    gate_up = matmul(normed_two_low, gate_up_full)
+    activated, pull_swiglu = jax.vjp(swiglu, gate_up)
+    act_low = activated.astype(jnp.bfloat16)
+    block_out = (residual + matmul(act_low, down_full)).astype(jnp.bfloat16)
+    grad_out = out_grad.reshape(flat_rows, MODEL_WIDTH)
+    grad_down = left_t(act_low, grad_out)
+    (grad_gate_up,) = pull_swiglu(right_t(grad_out, down_full))
+    grad_gate_up_low = grad_gate_up.astype(jnp.bfloat16)
+    grad_gate_up_w = left_t(normed_two_low, grad_gate_up_low)
+    hw = MODEL_WIDTH // 2
+    sum_down = scatter_sum(grad_down[:, :hw], grad_down[:, hw:])
+    sum_gate_up = scatter_sum(grad_gate_up_w[:, :FF], grad_gate_up_w[:, FF:])
+    grad_resid_norm, grad_gain_two = pull_norm_two(right_t(grad_gate_up_low, gate_up_full))
+    grad_resid = grad_out.astype(jnp.float32) + grad_resid_norm
+    grad_branch = grad_resid.astype(jnp.bfloat16)
+    grad_attn_w = left_t(attn_low, grad_branch)
+    grad_mix_out_w = left_t(normed_mix_low, grad_branch)
+    count = lax.axis_size(BOTH)
+    out_w = jnp.concatenate(
+        [
+            grad_mix_out_w.astype(jnp.bfloat16).reshape(count, -1, MODEL_WIDTH),
+            grad_attn_w.astype(jnp.bfloat16).reshape(count, -1, MODEL_WIDTH),
+        ],
+        1,
+    ).reshape(-1, MODEL_WIDTH)
+    sum_out = scatter_sum(out_w[:, :hw], out_w[:, hw:])
+    grad_attn = right_t(grad_branch, attn_out_full).astype(jnp.bfloat16)
+    grad_attn = grad_attn.reshape(seqs, local_rows, QUERY_HEADS, HEAD_WIDTH)
+    grad_mixer, grad_gate_z, grad_mix_gain = pull_gated(right_t(grad_branch, mix_out_full))
+    grad_gate_z_low = grad_gate_z.astype(jnp.bfloat16)
+    grad_gate_z_w = left_t(normed_low, grad_gate_z_low)
+    sum_z = scatter_sum(grad_gate_z_w[:, : DI // 2], grad_gate_z_w[:, DI // 2 :])
+    grad_mixer = grad_mixer.reshape(seqs, local_rows, DI)
+    rows_out = []
+    totals = None
+    for s in range(seqs):
+        grad_query, grad_kv = attend_backward(
+            queries[s], key_value_rows[s], seg_block[s], query_pos, log_sums[s], attns[s], grad_attn[s]
         )
-        raw_step = matmul(normed_low, step_full).reshape(local_sequence, local_rows, H)
-        queries = (
-            matmul(normed_low, query_full)
-            .astype(jnp.bfloat16)
-            .reshape(local_sequence, local_rows, QUERY_HEADS * HEAD_WIDTH)
-        )
-        key_value_rows = (
-            matmul(normed_low, keyval_full)
-            .astype(jnp.bfloat16)
-            .reshape(local_sequence, local_rows, 2 * KEY_VALUE_HEADS * HEAD_WIDTH)
-        )
-        seq_index = 0
-        mixer_out, saved_terms = mixer_forward(
-            conv_in[seq_index],
-            seg_block[seq_index],
-            raw_step[seq_index],
-            kernel_f,
-            offset_f,
-            step_bias,
-            decay_log,
-            skip_gain,
-        )
-        saved_list = [saved_terms]
-        attn_vals, log_sum = attend_forward(
-            queries[seq_index], key_value_rows[seq_index], seg_block[seq_index], query_pos
-        )
-        attn_list = [attn_vals]
-        lse_list = [log_sum]
-        normed_mix, pull_gated = jax.vjp(
-            gated_norm, mixer_out, gate_z, mix_gain_full.astype(jnp.float32)
-        )
-        normed_mix_low = normed_mix.astype(jnp.bfloat16)
-        mamba_part = matmul(normed_mix_low, mix_out_full)
-        attn_low = attn_list[0].astype(jnp.bfloat16).reshape(flat_rows, QUERY_HEADS * HEAD_WIDTH)
-        attn_part = matmul(attn_low, attn_out_full)
-        residual = tokens + mamba_part + attn_part
-        normed_two, pull_norm_two = jax.vjp(rms_gain, residual, gain_two.astype(jnp.float32))
-        normed_two_low = normed_two.astype(jnp.bfloat16)
-        gate_up = matmul(normed_two_low, gate_up_full)
-        activated, pull_swiglu = jax.vjp(swiglu, gate_up)
-        act_low = activated.astype(jnp.bfloat16)
-        block_out = residual + matmul(act_low, down_full)
-        out_list.append(
-            block_out.astype(jnp.bfloat16).reshape(local_sequence, local_rows, MODEL_WIDTH)
-        )
-        back_weights = (
-            lax.all_gather(w_gate_z, ("dp", "fsdp"), axis=0, tiled=True),
-            lax.all_gather(w_xbc, ("dp", "fsdp"), axis=0, tiled=True),
-            lax.all_gather(w_step, ("dp", "fsdp"), axis=0, tiled=True),
-            lax.all_gather(w_mix_out, ("dp", "fsdp"), axis=0, tiled=True),
-            lax.all_gather(w_query, ("dp", "fsdp"), axis=0, tiled=True),
-            lax.all_gather(key_value_weight, ("dp", "fsdp"), axis=0, tiled=True),
-            lax.all_gather(w_attn_out, ("dp", "fsdp"), axis=0, tiled=True),
-            lax.all_gather(w_gate_up, ("dp", "fsdp"), axis=0, tiled=True),
-            lax.all_gather(w_down, ("dp", "fsdp"), axis=0, tiled=True),
-        )
-        (
-            gate_z_bwd,
-            xbc_bwd,
-            step_bwd,
-            mix_out_bwd,
-            query_bwd,
-            keyval_bwd,
-            attn_out_bwd,
-            gate_up_bwd,
-            down_bwd,
-        ) = back_weights
-        grad_out = out_grad[micro_step].reshape(flat_rows, MODEL_WIDTH)
-        grad_down = left_t(act_low, grad_out)
-        (grad_gate_up,) = pull_swiglu(right_t(grad_out, down_bwd))
-        grad_gate_up_low = grad_gate_up.astype(jnp.bfloat16)
-        grad_gate_up_w = left_t(normed_two_low, grad_gate_up_low)
-        grad_resid_norm, grad_gain_two = pull_norm_two(right_t(grad_gate_up_low, gate_up_bwd))
-        grad_resid = grad_out.astype(jnp.float32) + grad_resid_norm
-        grad_branch = grad_resid.astype(jnp.bfloat16)
-        grad_attn_w = left_t(attn_low, grad_branch)
-        grad_mix_out_w = left_t(normed_mix_low, grad_branch)
-        gradient_attention_values = (
-            right_t(grad_branch, attn_out_bwd)
-            .astype(jnp.bfloat16)
-            .reshape(local_sequence, local_rows, QUERY_HEADS, HEAD_WIDTH)
-        )
-        grad_mixer_all, grad_gate_z, grad_mix_gain = pull_gated(right_t(grad_branch, mix_out_bwd))
-        grad_mixer_seq = grad_mixer_all.reshape(local_sequence, local_rows, DI)
-        seq_index = 0
-        grad_query_low, grad_kv = attend_backward(
-            queries[seq_index],
-            key_value_rows[seq_index],
-            seg_block[seq_index],
-            query_pos,
-            lse_list[seq_index],
-            attn_list[seq_index],
-            gradient_attention_values[seq_index],
-        )
-        conv_seq, raw_seq, kernel_part, offset_part, bias_part, decay_part, skip_part = (
-            mixer_backward(saved_list[seq_index], grad_mixer_seq[seq_index])
-        )
-        bias_total = bias_total + bias_part
-        decay_total = decay_total + decay_part
-        skip_total = skip_total + skip_part
-        grad_raw_low = raw_seq.astype(jnp.bfloat16)
-        grad_gate_z_low = grad_gate_z.astype(jnp.bfloat16)
-        grad_normed = (
-            right_t(grad_gate_z_low, gate_z_bwd)
-            + right_t(conv_seq, xbc_bwd)
-            + right_t(grad_raw_low, step_bwd)
-            + right_t(grad_query_low, query_bwd)
-            + right_t(grad_kv, keyval_bwd)
-        )
-        grad_tokens, grad_gain_one = pull_norm_one(grad_normed)
-        grad_in_list.append(
-            (grad_resid + grad_tokens).reshape(local_sequence, local_rows, MODEL_WIDTH)
-        )
-        grad_gate_z_w = left_t(normed_low, grad_gate_z_low)
-        grad_xbc_w = left_t(normed_low, conv_seq)
-        grad_step_w = left_t(normed_low, grad_raw_low)
-        grad_query_w = left_t(normed_low, grad_query_low)
-        grad_keyval_w = left_t(normed_low, grad_kv)
-        owned_parts = (
-            lax.psum_scatter(grad_gain_one, ("dp", "fsdp"), scatter_dimension=0, tiled=True),
-            lax.psum_scatter(grad_gate_z_w, ("dp", "fsdp"), scatter_dimension=0, tiled=True),
-            lax.psum_scatter(grad_xbc_w, ("dp", "fsdp"), scatter_dimension=0, tiled=True),
-            lax.psum_scatter(grad_step_w, ("dp", "fsdp"), scatter_dimension=0, tiled=True),
-            lax.psum_scatter(kernel_part, ("dp", "fsdp"), scatter_dimension=1, tiled=True),
-            lax.psum_scatter(offset_part, ("dp", "fsdp"), scatter_dimension=0, tiled=True),
-            lax.psum_scatter(grad_mix_gain, ("dp", "fsdp"), scatter_dimension=0, tiled=True),
-            lax.psum_scatter(grad_mix_out_w, ("dp", "fsdp"), scatter_dimension=0, tiled=True),
-            lax.psum_scatter(grad_query_w, ("dp", "fsdp"), scatter_dimension=0, tiled=True),
-            lax.psum_scatter(grad_keyval_w, ("dp", "fsdp"), scatter_dimension=0, tiled=True),
-            lax.psum_scatter(grad_attn_w, ("dp", "fsdp"), scatter_dimension=0, tiled=True),
-            lax.psum_scatter(grad_gain_two, ("dp", "fsdp"), scatter_dimension=0, tiled=True),
-            lax.psum_scatter(grad_gate_up_w, ("dp", "fsdp"), scatter_dimension=0, tiled=True),
-            lax.psum_scatter(grad_down, ("dp", "fsdp"), scatter_dimension=0, tiled=True),
-        )
-        shard_total = (
-            owned_parts if shard_total is None else jax.tree.map(jnp.add, shard_total, owned_parts)
-        )
-    head_sums = lax.psum((bias_total, decay_total, skip_total), ("dp", "fsdp"))
-    hidden_out = jnp.stack(out_list)
-    input_grad = jnp.stack(grad_in_list)
+        conv_seq, raw_seq, *parts = mixer_backward(saved[s], grad_mixer[s])
+        totals = parts if totals is None else jax.tree.map(jnp.add, totals, parts)
+        raw_low = jnp.pad(raw_seq.astype(jnp.bfloat16), ((0, 0), (0, 128 - H)))
+        rows_out.append(jnp.concatenate([conv_seq, raw_low, grad_query, grad_kv], 1))
+    kernel_part, offset_part, bias_part, decay_part, skip_part = totals
+    grad_first = jnp.concatenate(rows_out)
+    grad_first = jnp.pad(grad_first, ((0, 0), (0, first_full.shape[1] - grad_first.shape[1])))
+    grad_first_w = left_t(normed_low, grad_first)
+    h1 = grad_first.shape[1] // 2
+    sum_first = scatter_sum(grad_first_w[:, :h1], grad_first_w[:, h1:])
+    grad_normed = right_t(grad_gate_z_low, z_full) + right_t(grad_first, first_full)
+    grad_tokens, grad_gain_one = pull_norm_one(grad_normed)
+    input_grad = grad_resid + grad_tokens
+    parts = [
+        grad_gain_one.reshape(count, -1),
+        grad_gain_two.reshape(count, -1),
+        grad_mix_gain.reshape(count, -1),
+        offset_part.reshape(count, -1),
+        kernel_part.reshape(KC, count, -1).transpose(1, 0, 2).reshape(count, -1),
+    ]
+    small_grads = jnp.concatenate(parts, 1)
+    small_grads = jnp.pad(small_grads, ((0, 0), (0, small_pad)))
+    own_small = lax.psum_scatter(small_grads, BOTH, scatter_dimension=0, tiled=True)[0]
+    own = []
+    at = 0
+    for size in sizes:
+        own.append(own_small[at : at + size])
+        at += size
+    head_sums = lax.psum(jnp.stack([bias_part, decay_part, skip_part]), BOTH)
+    sum_first = jnp.concatenate([sum_first[0], sum_first[1]], 1)
+    rm = w_mix_out.shape[0]
+    sum_out = jnp.concatenate([sum_out[0], sum_out[1]], 1)
     return (
-        hidden_out,
-        input_grad,
-        shard_total[0],
-        shard_total[1],
-        shard_total[2],
-        shard_total[3],
-        shard_total[4],
-        shard_total[5],
+        block_out.reshape(hidden_in.shape),
+        input_grad.reshape(hidden_in.shape),
+        own[0],
+        jnp.concatenate([sum_z[0], sum_z[1]], 1),
+        sum_first[:, :conv_width],
+        sum_first[:, conv_width : conv_width + H],
+        own[4].reshape(KC, -1),
+        own[3],
         head_sums[0],
         head_sums[1],
         head_sums[2],
-        shard_total[6],
-        shard_total[7],
-        shard_total[8],
-        shard_total[9],
-        shard_total[10],
-        shard_total[11],
-        shard_total[12],
-        shard_total[13],
+        own[2],
+        sum_out[:rm],
+        sum_first[:, q0 : q0 + query_width],
+        sum_first[:, k0 : k0 + kv_width],
+        sum_out[rm:],
+        own[1],
+        jnp.concatenate([sum_gate_up[0], sum_gate_up[1]], 1),
+        jnp.concatenate([sum_down[0], sum_down[1]], 1),
     )
 
 

time: 1970 us -> 1100 us (0.56)
  waiting for transfers between devices: 1150 us -> 229 us
  blocking collectives: 279 us -> 182 us
  starting transfers between devices: 15.6 us -> 103 us
  matrix products: 311 us -> 241 us
  local copies, waits for them, and re-layouts: 94.6 us -> 160 us
  other arithmetic: 83.4 us -> 133 us
    reduce_scatter x8 -> x0, waiting for transfers between devices: 1050 us -> none  [the longest x1 201 us: per_device(): lax.psum_scatter(grad_gate_up_w, ('dp', 'fsdp'), scatter_dimension=0, til...]
    ppermute x0 -> x90, waiting for transfers between devices: none -> 124 us  [exchange(): return lax.ppermute(block, BOTH, [(i, i ^ 1 << bit) for i in range(count)])]
    unnamed x23 -> x8, waiting for transfers between devices: 4.08 us -> 103 us
    all_gather x7 -> x0, waiting for transfers between devices: 92.2 us -> none  [the longest x1 50.7 us: per_device(): lax.all_gather(w_down, ('dp', 'fsdp'), axis=0, tiled=True)]
    ppermute x0 -> x90, starting transfers between devices: none -> 88.7 us  [exchange(): return lax.ppermute(block, BOTH, [(i, i ^ 1 << bit) for i in range(count)])]
    unnamed x2 -> x0, blocking collectives: 82 us -> none
    all_gather x3 -> x1, blocking collectives: 112 us -> 48.1 us  [per_device(): lax.all_gather(small, BOTH, axis=0, tiled=True).astype(jnp.float32)]
    psum x0 -> x1, blocking collectives: none -> 39.2 us  [per_device(): head_sums = lax.psum(jnp.stack([bias_part, decay_part, skip_part]), BOTH)]
  transfers between devices with their start and end apart: 28 -> 103, of which waited for: 11 -> 32; matrix products, arithmetic and copies ran while one was open for 21% -> 31% of each run, Pallas kernels for 0% -> 1%
where the time goes in v1:
time: 1100 us; the launch traced here: 1090 us
  matrix products  241 us (22%)
  waiting for transfers between devices  229 us (21%)
  blocking collectives  182 us (17%)
  local copies, waits for them, and re-layouts  160 us (15%)
  other arithmetic  133 us (12%)
  starting transfers between devices  103 us (9%)
  between operations  23.4 us (2%)
  Pallas kernels  15.3 us (1%)
    ppermute x90, waiting for transfers between devices, exchange(): return lax.ppermute(block, BOTH, [(i, i ^ 1 << bit) for i in range(count)])  124 us
    unnamed x8, waiting for transfers between devices  103 us
    ppermute x90, starting transfers between devices, exchange(): return lax.ppermute(block, BOTH, [(i, i ^ 1 << bit) for i in range(count)])  88.7 us
    dot_general x6, matrix products, mixer_output(): inside = jnp.einsum('hts,shp->thp', mixing, inputs, precision=HIGHEST)  53.8 us
    unnamed x725, local copies, waits for them, and re-layouts  48.8 us
    all_gather x1, blocking collectives, per_device(): lax.all_gather(small, BOTH, axis=0, tiled=True).astype(jnp.float32)  48.1 us
    all_gather x2, blocking collectives, entering_2(): lax.all_gather(a.astype(kind), axis)  39.4 us
    psum x1, blocking collectives, per_device(): head_sums = lax.psum(jnp.stack([bias_part, decay_part, skip_part]), BOTH)  39.2 us
  transfers between devices with their start and end apart: 103, of which 32 were waited for; matrix products, arithmetic and copies ran while one was open for 31% of the time, Pallas kernels for 1%

profile of v1, /device:TPU:8, one launch (start us, length us, event | category | flops | bytes accessed | tf_op | source)
XLA Modules:
  0.0 1086.1 jit_solution(942593523995864706)
XLA Ops:
  21.9 48.1 %all-gather.11 = bf16[32,1,512]{2,1,0:T(2,128)(2,1)S(1)} all-gather(bf16[1,1,512]{2,1,0:T(2,128)(2,1)S(1)} %reshape.1279), channel_id=2, replica_groups=mesh['dp'=8,'fsdp'=4] {'dp','fsdp'}, dimensions={0}, use_global_device_ids=true | all-gather | bytes 33792 | tf_op jit(solution)/shard_map/all_gather | solution.py:576
  71.6 5.9 all-gather.7
  77.6 5.1 all-gather.8
  120.3 4.1 collective-permute-start.13
  125.5 4.3 collective-permute-start.17
  134.0 4.7 collective-permute-done.35
  147.4 15.2 %all-reduce.44 = (s32[4]{0:T(128)}, s32[4]{0:T(128)}, s32[4]{0:T(128)}, s32[4]{0:T(128)}) all-reduce(s32[4]{0:T(128)S(1)} %bitcast_dynamic-update-slice_fusion.1, s32[4]{0:T(128)S(1)} %bitcast_dynamic-update-slice_fusion, s32[4]{0:T(128)S(1)} %bitcast_dynamic-update-slice_fusion.3, ...), channel_id=7, replica_groups=mesh['dp'=8,'fsdp'=4] {'fsdp'}, use_global_device_ids=true, to_apply=%add.41 | all-reduce | flops 16 | bytes 128 | tf_op jit(solution)/shard_map/all_gather | solution.py:35
  172.2 9.6 collective-permute-done.47.refs_1_
  227.2 3.9 assemble.7
  244.2 5.0 fusion.403
  252.0 11.0 %all_gather.85 = bf16[1024,256]{1,0:T(8,128)(2,1)S(1)} all-gather(bf16[256,256]{1,0:T(8,128)(2,1)S(1)} %get-tuple-element.628), channel_id=1, replica_groups=mesh['dp'=8,'fsdp'=4] {'fsdp'}, dimensions={0}, use_global_device_ids=true | all-gather | bytes 655360 | tf_op jit(solution)/shard_map/all_gather | solution.py:286
  264.0 4.6 fusion.31
  269.2 7.8 all_gather.83
  280.1 4.6 fusion.30
  292.3 4.6 fusion.10
  307.9 4.0 fusion.115
  321.5 5.6 fusion.41
  329.4 5.6 fusion.43
  346.1 5.0 all-gather.13
  351.3 5.0 all-gather.12
  360.5 4.2 assemble.8
  373.1 9.7 fusion.118
  388.5 8.4 fusion.119
  400.0 6.2 multiply_reduce_fusion.6
  408.9 7.8 fusion.373
  416.8 7.0 bitcast_multiply_fusion.1
  423.7 10.8 multiply_reduce_fusion.7
  441.9 4.1 fusion.55
  456.4 6.4 fusion.167
  462.8 5.1 fusion.1
  471.7 10.4 fusion.52
  482.1 7.0 bitcast_add_fusion.1
  492.4 11.7 %fusion.50 = (f32[24,256]{1,0:T(8,128)}, f32[24,256]{1,0:T(8,128)}, f32[24,256]{1,0:T(8,128)}, f32[256,256]{1,0:T(8,128)}) fusion(f32[24,256]{1,0:T(8,128)S(1)} %copy-done.268, f32[256,256]{1,0:T(8,128)} %fusion.295, f32[24,256]{1,0:T(8,128)} %get-tuple-element.708, pred[256,256]{1,0:T(8,128)(4,1)} %fusion.259, f32[24,64,256]{2,1,0:T(8,128)} %bitcast.1087, ...), kind=kOutput, calls=%fused_computation.86 | convolution fusion | flops 1228322816 | bytes 3858432 | tf_op jit(solution)/shard_map/transpose(jvp(hts,shp->thp))/dot_general | solution.py:148
  505.1 6.6 bitcast_add_fusion.2
  511.7 6.4 fusion.170
  518.1 5.1 fusion.3
  533.4 34.3 %all-gather.15 = bf16[4,1,24]{2,1,0:T(2,128)(2,1)S(1)} all-gather(bf16[1,1,24]{2,1,0:T(2,128)(2,1)S(1)} %bitcast.1184), channel_id=1, replica_groups=mesh['dp'=8,'fsdp'=4] {'fsdp'}, dimensions={0}, use_global_device_ids=true | all-gather | bytes 240 | tf_op jit(solution)/shard_map/all_gather | solution.py:59
  568.5 5.0 all-gather.14
  581.1 3.8 reduce-window.50
  608.2 8.7 convolution_convert_fusion
  620.8 4.1 constant_dynamic-slice_fusion.7
  646.1 6.9 add_convert_fusion.1
  672.3 8.1 collective-permute-done.73
  684.9 6.3 collective-permute-done.89
  693.1 5.0 collective-permute-done.92
  698.9 4.8 collective-permute-done.74
  728.0 4.0 collective-permute-done.95
  732.9 3.9 while.61
  736.8 4.0 broadcast_multiply_fusion.2
  745.5 4.8 broadcast_multiply_fusion.3
  764.0 4.5 multiply_reduce_fusion.13
  786.3 39.2 %psum.7 = f32[3,24]{1,0:T(4,128)S(1)} all-reduce(f32[3,24]{1,0:T(4,128)S(1)} %pad_maximum_fusion.32), channel_id=1, replica_groups=mesh['dp'=8,'fsdp'=4] {'dp','fsdp'}, use_global_device_ids=true, to_apply=%region_76.78 | all-reduce | flops 72 | bytes 576 | tf_op jit(solution)/shard_map/psum | solution.py:685
  834.7 7.4 fusion.86
  842.2 5.4 fusion.91
  854.6 5.2 convolution_convert_fusion.1
  877.9 103.0 %all-reduce.47.cloned.1.call-done = f32[32,512]{1,0:T(8,128)} async-done(((f32[32,512]{1,0:T(8,128)}), f32[32,512]{1,0:T(8,128)}) %all-reduce.47.cloned.1.call-update) | async-done | bytes 65552
  996.5 7.6 collective-permute-done.57
  1005.1 5.8 collective-permute-done.60
  1013.6 5.3 collective-permute-done.85
  1024.9 9.9 collective-permute-done.62
  1036.4 6.4 collective-permute-done.63
  1047.2 4.9 collective-permute-done.87
  1054.8 5.1 collective-permute-done.66
  1064.0 5.4 collective-permute-done.70
  (1310 shorter events, 470.2 us)
Async XLA Ops:
  7.3 360.7 %all-gather.23.cloned.1.call-start = ((), (), s32[]{:S(2)}) async-start(), calls=%async_computation.5 | async-start | bytes 1966080 | tf_op jit(solution)/shard_map/all_gather | solution.py:35
  9.2 82.8 %collective-permute-start.24 = (bf16[1,2,64,512]{3,2,0,1:T(8,128)(2,1)S(1)}, bf16[1,2,64,512]{3,2,0,1:T(8,128)(2,1)S(1)}, u32[]{:S(2)}, u32[]{:S(2)}) collective-permute-start(bf16[1,2,64,512]{3,2,0,1:T(8,128)(2,1)S(1)} %maximum_bitcast_fusion.2), channel_id=1, source_target_pairs={{0,16},{1,17},{2,18},{3,19},{4,20},{5,21},{6,22},{7,23},{8,24},{9,... | collective-permute-start | bytes 393224 | tf_op jit(solution)/shard_map/ppermute | solution.py:376
  14.5 79.7 %collective-permute-start = (bf16[1,2,32,1408]{3,2,0,1:T(8,128)(2,1)S(1)}, bf16[1,2,32,1408]{3,2,0,1:T(8,128)(2,1)S(1)}, u32[]{:S(2)}, u32[]{:S(2)}) collective-permute-start(bf16[1,2,32,1408]{3,2,0,1:T(8,128)(2,1)S(1)} %maximum_bitcast_fusion.1), channel_id=1, source_target_pairs={{0,16},{1,17},{2,18},{3,19},{4,20},{5,21},{6,22},{7,23},{8,24},{9,... | collective-permute-start | bytes 540680 | tf_op jit(solution)/shard_map/ppermute | solution.py:376
  15.8 76.1 %collective-permute-start.14 = (bf16[1,2,32,768]{3,2,0,1:T(8,128)(2,1)S(1)}, bf16[1,2,32,768]{3,2,0,1:T(8,128)(2,1)S(1)}, u32[]{:S(2)}, u32[]{:S(2)}) collective-permute-start(bf16[1,2,32,768]{3,2,0,1:T(8,128)(2,1)S(1)} %maximum_bitcast_fusion.4), channel_id=1, source_target_pairs={{0,16},{1,17},{2,18},{3,19},{4,20},{5,21},{6,22},{7,23},{8,24},{9,... | collective-permute-start | bytes 294920 | tf_op jit(solution)/shard_map/ppermute | solution.py:376
  18.5 77.8 %collective-permute-start.34 = (bf16[1,2,32,2048]{3,2,0,1:T(8,128)(2,1)S(1)}, bf16[1,2,32,2048]{3,2,0,1:T(8,128)(2,1)S(1)}, u32[]{:S(2)}, u32[]{:S(2)}) collective-permute-start(bf16[1,2,32,2048]{3,2,0,1:T(8,128)(2,1)S(1)} %maximum_bitcast_fusion), channel_id=1, source_target_pairs={{0,16},{1,17},{2,18},{3,19},{4,20},{5,21},{6,22},{7,23},{8,24},{9,... | collective-permute-start | bytes 786440 | tf_op jit(solution)/shard_map/ppermute | solution.py:376
  19.0 75.1 %collective-permute-start.44 = (bf16[1,2,64,512]{3,2,0,1:T(8,128)(2,1)S(1)}, bf16[1,2,64,512]{3,2,0,1:T(8,128)(2,1)S(1)}, u32[]{:S(2)}, u32[]{:S(2)}) collective-permute-start(bf16[1,2,64,512]{3,2,0,1:T(8,128)(2,1)S(1)} %maximum_bitcast_fusion.3), channel_id=1, source_target_pairs={{0,16},{1,17},{2,18},{3,19},{4,20},{5,21},{6,22},{7,23},{8,24},{9,... | collective-permute-start | bytes 393224 | tf_op jit(solution)/shard_map/ppermute | solution.py:376
  94.1 16.8 %collective-permute-start.45 = (bf16[2,2,64,512]{3,2,0,1:T(8,128)(2,1)S(1)}, bf16[2,2,64,512]{3,2,0,1:T(8,128)(2,1)S(1)}, u32[]{:S(2)}, u32[]{:S(2)}) collective-permute-start(bf16[2,2,64,512]{3,2,0,1:T(8,128)(2,1)S(1)} %pad_maximum_fusion.26), channel_id=1, source_target_pairs={{0,8},{1,9},{2,10},{3,11},{4,12},{5,13},{6,14},{7,15},{8,0},{9,1},... | collective-permute-start | bytes 786440 | tf_op jit(solution)/shard_map/ppermute | solution.py:376
  94.3 23.8 %collective-permute-start.1 = (bf16[2,2,32,1408]{3,2,0,1:T(8,128)(2,1)S(1)}, bf16[2,2,32,1408]{3,2,0,1:T(8,128)(2,1)S(1)}, u32[]{:S(2)}, u32[]{:S(2)}) collective-permute-start(bf16[2,2,32,1408]{3,2,0,1:T(8,128)(2,1)S(1)} %pad_maximum_fusion.22), channel_id=1, source_target_pairs={{0,8},{1,9},{2,10},{3,11},{4,12},{5,13},{6,14},{7,15},{8,0},{9,1},... | collective-permute-start | bytes 1081352 | tf_op jit(solution)/shard_map/ppermute | solution.py:376
  105.4 20.1 %collective-permute-start.26 = (bf16[4,64,512]{2,1,0:T(8,128)(2,1)S(1)}, bf16[4,64,512]{2,1,0:T(8,128)(2,1)S(1)}, u32[]{:S(2)}, u32[]{:S(2)}) collective-permute-start(bf16[4,64,512]{2,1,0:T(8,128)(2,1)S(1)} %get-tuple-element.667), channel_id=1, source_target_pairs={{0,4},{1,5},{2,6},{3,7},{4,0},{5,1},{6,2},{7,3},{8,12},{9,13},{10,... | collective-permute-start | bytes 786440 | tf_op jit(solution)/shard_map/ppermute | solution.py:376
  110.9 18.9 %collective-permute-start.30 = (bf16[4,64,512]{2,1,0:T(8,128)(2,1)S(1)}, bf16[4,64,512]{2,1,0:T(8,128)(2,1)S(1)}, u32[]{:S(2)}, u32[]{:S(2)}) collective-permute-start(bf16[4,64,512]{2,1,0:T(8,128)(2,1)S(1)} %get-tuple-element.666), channel_id=1, source_target_pairs={{0,2},{1,3},{2,0},{3,1},{4,6},{5,7},{6,4},{7,5},{8,10},{9,11},{10,... | collective-permute-start | bytes 786440 | tf_op jit(solution)/shard_map/ppermute | solution.py:376
  112.8 17.1 %collective-permute-start.46 = (bf16[4,64,512]{2,1,0:T(8,128)(2,1)S(1)}, bf16[4,64,512]{2,1,0:T(8,128)(2,1)S(1)}, u32[]{:S(2)}, u32[]{:S(2)}) collective-permute-start(bf16[4,64,512]{2,1,0:T(8,128)(2,1)S(1)} %get-tuple-element.661), channel_id=1, source_target_pairs={{0,4},{1,5},{2,6},{3,7},{4,0},{5,1},{6,2},{7,3},{8,12},{9,13},{10,... | collective-permute-start | bytes 786440 | tf_op jit(solution)/shard_map/ppermute | solution.py:376
  115.2 17.0 %collective-permute-start.50 = (bf16[4,64,512]{2,1,0:T(8,128)(2,1)S(1)}, bf16[4,64,512]{2,1,0:T(8,128)(2,1)S(1)}, u32[]{:S(2)}, u32[]{:S(2)}) collective-permute-start(bf16[4,64,512]{2,1,0:T(8,128)(2,1)S(1)} %get-tuple-element.660), channel_id=1, source_target_pairs={{0,2},{1,3},{2,0},{3,1},{4,6},{5,7},{6,4},{7,5},{8,10},{9,11},{10,... | collective-permute-start | bytes 786440 | tf_op jit(solution)/shard_map/ppermute | solution.py:376
  125.5 16.1 %collective-permute-start.17 = (bf16[8,32,768]{2,1,0:T(8,128)(2,1)S(1)}, bf16[8,32,768]{2,1,0:T(8,128)(2,1)S(1)}, u32[]{:S(2)}, u32[]{:S(2)}) collective-permute-start(bf16[8,32,768]{2,1,0:T(8,128)(2,1)S(1)} %pad_maximum_fusion.20.refs_0_), channel_id=1, source_target_pairs={{0,2},{1,3},{2,0},{3,1},{4,6},{5,7},{6,4},{7,5},{8,10},{9,11},{10,... | collective-permute-start | bytes 1179656 | tf_op jit(solution)/shard_map/ppermute | solution.py:376
  138.7 29.0 %collective-permute-start.27 = (bf16[8,64,512]{2,1,0:T(8,128)(2,1)S(1)}, bf16[8,64,512]{2,1,0:T(8,128)(2,1)S(1)}, u32[]{:S(2)}, u32[]{:S(2)}) collective-permute-start(bf16[8,64,512]{2,1,0:T(8,128)(2,1)S(1)} %pad_maximum_fusion.9.refs_0_), channel_id=1, source_target_pairs={{0,2},{1,3},{2,0},{3,1},{4,6},{5,7},{6,4},{7,5},{8,10},{9,11},{10,... | collective-permute-start | bytes 1572872 | tf_op jit(solution)/shard_map/ppermute | solution.py:376
  141.6 25.6 %collective-permute-start.2 = (bf16[4,32,1408]{2,1,0:T(8,128)(2,1)}, bf16[4,32,1408]{2,1,0:T(8,128)(2,1)}, u32[]{:S(2)}, u32[]{:S(2)}) collective-permute-start(bf16[4,32,1408]{2,1,0:T(8,128)(2,1)} %get-tuple-element.655), channel_id=1, source_target_pairs={{0,4},{1,5},{2,6},{3,7},{4,0},{5,1},{6,2},{7,3},{8,12},{9,13},{10,... | collective-permute-start | bytes 1081352 | tf_op jit(solution)/shard_map/ppermute | solution.py:376
  144.8 22.5 %collective-permute-start.6 = (bf16[4,32,1408]{2,1,0:T(8,128)(2,1)}, bf16[4,32,1408]{2,1,0:T(8,128)(2,1)}, u32[]{:S(2)}, u32[]{:S(2)}) collective-permute-start(bf16[4,32,1408]{2,1,0:T(8,128)(2,1)} %get-tuple-element.654), channel_id=1, source_target_pairs={{0,2},{1,3},{2,0},{3,1},{4,6},{5,7},{6,4},{7,5},{8,10},{9,11},{10,... | collective-permute-start | bytes 1081352 | tf_op jit(solution)/shard_map/ppermute | solution.py:376
  144.8 24.3 %collective-permute-start.28 = (bf16[8,64,512]{2,1,0:T(8,128)(2,1)S(1)}, bf16[8,64,512]{2,1,0:T(8,128)(2,1)S(1)}, u32[]{:S(2)}, u32[]{:S(2)}) collective-permute-start(bf16[8,64,512]{2,1,0:T(8,128)(2,1)S(1)} %pad_maximum_fusion.9.refs_0_), channel_id=1, source_target_pairs={{0,1},{1,0},{2,3},{3,2},{4,5},{5,4},{6,7},{7,6},{8,9},{9,8},{10,11... | collective-permute-start | bytes 1572872 | tf_op jit(solution)/shard_map/ppermute | solution.py:376
  146.4 25.2 %collective-permute-start.31 = (bf16[8,64,512]{2,1,0:T(8,128)(2,1)S(1)}, bf16[8,64,512]{2,1,0:T(8,128)(2,1)S(1)}, u32[]{:S(2)}, u32[]{:S(2)}) collective-permute-start(bf16[8,64,512]{2,1,0:T(8,128)(2,1)S(1)} %pad_maximum_fusion.10.refs_4_), channel_id=1, source_target_pairs={{0,4},{1,5},{2,6},{3,7},{4,0},{5,1},{6,2},{7,3},{8,12},{9,13},{10,... | collective-permute-start | bytes 1572872 | tf_op jit(solution)/shard_map/ppermute | solution.py:376
  169.1 15.1 %collective-permute-start.51 = (bf16[8,64,512]{2,1,0:T(8,128)(2,1)S(1)}, bf16[8,64,512]{2,1,0:T(8,128)(2,1)S(1)}, u32[]{:S(2)}, u32[]{:S(2)}) collective-permute-start(bf16[8,64,512]{2,1,0:T(8,128)(2,1)S(1)} %pad_maximum_fusion.15.refs_4_), channel_id=1, source_target_pairs={{0,4},{1,5},{2,6},{3,7},{4,0},{5,1},{6,2},{7,3},{8,12},{9,13},{10,... | collective-permute-start | bytes 1572872 | tf_op jit(solution)/shard_map/ppermute | solution.py:376
  171.7 23.7 %collective-permute-start.36 = (bf16[4,32,2048]{2,1,0:T(8,128)(2,1)S(1)}, bf16[4,32,2048]{2,1,0:T(8,128)(2,1)S(1)}, u32[]{:S(2)}, u32[]{:S(2)}) collective-permute-start(bf16[4,32,2048]{2,1,0:T(8,128)(2,1)S(1)} %get-tuple-element.653), channel_id=1, source_target_pairs={{0,4},{1,5},{2,6},{3,7},{4,0},{5,1},{6,2},{7,3},{8,12},{9,13},{10,... | collective-permute-start | bytes 1572872 | tf_op jit(solution)/shard_map/ppermute | solution.py:376
  186.4 25.2 %collective-permute-start.3 = (bf16[8,32,1408]{2,1,0:T(8,128)(2,1)S(1)}, bf16[8,32,1408]{2,1,0:T(8,128)(2,1)}, u32[]{:S(2)}, u32[]{:S(2)}) collective-permute-start(bf16[8,32,1408]{2,1,0:T(8,128)(2,1)S(1)} %pad_maximum_fusion.6.refs_0_), channel_id=1, source_target_pairs={{0,2},{1,3},{2,0},{3,1},{4,6},{5,7},{6,4},{7,5},{8,10},{9,11},{10,... | collective-permute-start | bytes 2162696 | tf_op jit(solution)/shard_map/ppermute | solution.py:376
  188.9 22.8 %collective-permute-start.7 = (bf16[8,32,1408]{2,1,0:T(8,128)(2,1)S(1)}, bf16[8,32,1408]{2,1,0:T(8,128)(2,1)}, u32[]{:S(2)}, u32[]{:S(2)}) collective-permute-start(bf16[8,32,1408]{2,1,0:T(8,128)(2,1)S(1)} %pad_maximum_fusion.7.refs_4_), channel_id=1, source_target_pairs={{0,4},{1,5},{2,6},{3,7},{4,0},{5,1},{6,2},{7,3},{8,12},{9,13},{10,... | collective-permute-start | bytes 2162696 | tf_op jit(solution)/shard_map/ppermute | solution.py:376
  192.5 19.7 %collective-permute-start.29 = (bf16[8,64,512]{2,1,0:T(8,128)(2,1)S(1)}, bf16[8,64,512]{2,1,0:T(8,128)(2,1)}, u32[]{:S(2)}, u32[]{:S(2)}) collective-permute-start(bf16[8,64,512]{2,1,0:T(8,128)(2,1)S(1)} %copy-done.21), channel_id=1, source_target_pairs={{0,1},{1,0},{2,3},{3,2},{4,5},{5,4},{6,7},{7,6},{8,9},{9,8},{10,11... | collective-permute-start | bytes 1572872 | tf_op jit(solution)/shard_map/ppermute | solution.py:376
  195.5 16.8 %collective-permute-start.33 = (bf16[8,64,512]{2,1,0:T(8,128)(2,1)}, bf16[8,64,512]{2,1,0:T(8,128)(2,1)}, u32[]{:S(2)}, u32[]{:S(2)}) collective-permute-start(bf16[8,64,512]{2,1,0:T(8,128)(2,1)} %copy-done.25), channel_id=1, source_target_pairs={{0,1},{1,0},{2,3},{3,2},{4,5},{5,4},{6,7},{7,6},{8,9},{9,8},{10,11... | collective-permute-start | bytes 1572872 | tf_op jit(solution)/shard_map/ppermute | solution.py:376
  196.6 16.1 %collective-permute-start.49 = (bf16[8,64,512]{2,1,0:T(8,128)(2,1)}, bf16[8,64,512]{2,1,0:T(8,128)(2,1)S(1)}, u32[]{:S(2)}, u32[]{:S(2)}) collective-permute-start(bf16[8,64,512]{2,1,0:T(8,128)(2,1)} %collective-permute-done.47.refs_1_), channel_id=1, source_target_pairs={{0,1},{1,0},{2,3},{3,2},{4,5},{5,4},{6,7},{7,6},{8,9},{9,8},{10,11... | collective-permute-start | bytes 1572872 | tf_op jit(solution)/shard_map/ppermute | solution.py:376
  211.7 27.2 %collective-permute-start.4 = (bf16[8,32,1408]{2,1,0:T(8,128)(2,1)S(1)}, bf16[8,32,1408]{2,1,0:T(8,128)(2,1)S(1)}, u32[]{:S(2)}, u32[]{:S(2)}) collective-permute-start(bf16[8,32,1408]{2,1,0:T(8,128)(2,1)S(1)} %pad_maximum_fusion.6.refs_0_), channel_id=1, source_target_pairs={{0,1},{1,0},{2,3},{3,2},{4,5},{5,4},{6,7},{7,6},{8,9},{9,8},{10,11... | collective-permute-start | bytes 2162696 | tf_op jit(solution)/shard_map/ppermute | solution.py:376
  211.7 27.2 %collective-permute-start.8 = (bf16[8,32,1408]{2,1,0:T(8,128)(2,1)S(1)}, bf16[8,32,1408]{2,1,0:T(8,128)(2,1)S(1)}, u32[]{:S(2)}, u32[]{:S(2)}) collective-permute-start(bf16[8,32,1408]{2,1,0:T(8,128)(2,1)S(1)} %pad_maximum_fusion.7.refs_4_), channel_id=1, source_target_pairs={{0,1},{1,0},{2,3},{3,2},{4,5},{5,4},{6,7},{7,6},{8,9},{9,8},{10,11... | collective-permute-start | bytes 2162696 | tf_op jit(solution)/shard_map/ppermute | solution.py:376
  212.2 21.6 %collective-permute-start.53 = (bf16[8,64,512]{2,1,0:T(8,128)(2,1)}, bf16[8,64,512]{2,1,0:T(8,128)(2,1)S(1)}, u32[]{:S(2)}, u32[]{:S(2)}) collective-permute-start(bf16[8,64,512]{2,1,0:T(8,128)(2,1)} %copy-done.31), channel_id=1, source_target_pairs={{0,1},{1,0},{2,3},{3,2},{4,5},{5,4},{6,7},{7,6},{8,9},{9,8},{10,11... | collective-permute-start | bytes 1572872 | tf_op jit(solution)/shard_map/ppermute | solution.py:376
  212.3 28.7 %collective-permute-start.5 = (bf16[8,32,1408]{2,1,0:T(8,128)(2,1)}, bf16[8,32,1408]{2,1,0:T(8,128)(2,1)S(1)}, u32[]{:S(2)}, u32[]{:S(2)}) collective-permute-start(bf16[8,32,1408]{2,1,0:T(8,128)(2,1)} %collective-permute-done.3.refs_1_), channel_id=1, source_target_pairs={{0,1},{1,0},{2,3},{3,2},{4,5},{5,4},{6,7},{7,6},{8,9},{9,8},{10,11... | collective-permute-start | bytes 2162696 | tf_op jit(solution)/shard_map/ppermute | solution.py:376
  213.5 27.7 %collective-permute-start.9 = (bf16[8,32,1408]{2,1,0:T(8,128)(2,1)}, bf16[8,32,1408]{2,1,0:T(8,128)(2,1)S(1)}, u32[]{:S(2)}, u32[]{:S(2)}) collective-permute-start(bf16[8,32,1408]{2,1,0:T(8,128)(2,1)} %collective-permute-done.7.refs_5_), channel_id=1, source_target_pairs={{0,1},{1,0},{2,3},{3,2},{4,5},{5,4},{6,7},{7,6},{8,9},{9,8},{10,11... | collective-permute-start | bytes 2162696 | tf_op jit(solution)/shard_map/ppermute | solution.py:376
  233.8 101.4 %collective-permute-start.37 = (bf16[8,32,2048]{2,1,0:T(8,128)(2,1)S(1)}, bf16[8,32,2048]{2,1,0:T(8,128)(2,1)}, u32[]{:S(2)}, u32[]{:S(2)}) collective-permute-start(bf16[8,32,2048]{2,1,0:T(8,128)(2,1)S(1)} %pad_maximum_fusion.3.refs_0_), channel_id=1, source_target_pairs={{0,2},{1,3},{2,0},{3,1},{4,6},{5,7},{6,4},{7,5},{8,10},{9,11},{10,... | collective-permute-start | bytes 3145736 | tf_op jit(solution)/shard_map/ppermute | solution.py:376
  238.9 121.6 %collective-permute-start.38 = (bf16[8,32,2048]{2,1,0:T(8,128)(2,1)S(1)}, bf16[8,32,2048]{2,1,0:T(8,128)(2,1)}, u32[]{:S(2)}, u32[]{:S(2)}) collective-permute-start(bf16[8,32,2048]{2,1,0:T(8,128)(2,1)S(1)} %pad_maximum_fusion.3.refs_0_), channel_id=1, source_target_pairs={{0,1},{1,0},{2,3},{3,2},{4,5},{5,4},{6,7},{7,6},{8,9},{9,8},{10,11... | collective-permute-start | bytes 3145736 | tf_op jit(solution)/shard_map/ppermute | solution.py:376
  238.9 96.7 %collective-permute-start.41 = (bf16[8,32,2048]{2,1,0:T(8,128)(2,1)S(1)}, bf16[8,32,2048]{2,1,0:T(8,128)(2,1)}, u32[]{:S(2)}, u32[]{:S(2)}) collective-permute-start(bf16[8,32,2048]{2,1,0:T(8,128)(2,1)S(1)} %pad_maximum_fusion.4.refs_4_), channel_id=1, source_target_pairs={{0,4},{1,5},{2,6},{3,7},{4,0},{5,1},{6,2},{7,3},{8,12},{9,13},{10,... | collective-permute-start | bytes 3145736 | tf_op jit(solution)/shard_map/ppermute | solution.py:376
  241.0 119.5 %collective-permute-start.42 = (bf16[8,32,2048]{2,1,0:T(8,128)(2,1)S(1)}, bf16[8,32,2048]{2,1,0:T(8,128)(2,1)}, u32[]{:S(2)}, u32[]{:S(2)}) collective-permute-start(bf16[8,32,2048]{2,1,0:T(8,128)(2,1)S(1)} %pad_maximum_fusion.4.refs_4_), channel_id=1, source_target_pairs={{0,1},{1,0},{2,3},{3,2},{4,5},{5,4},{6,7},{7,6},{8,9},{9,8},{10,11... | collective-permute-start | bytes 3145736 | tf_op jit(solution)/shard_map/ppermute | solution.py:376
  284.8 17.1 %collective-permute-start.10 = (bf16[3,1792]{1,0:T(4,128)(2,1)}, bf16[3,1792]{1,0:T(4,128)(2,1)S(1)}, u32[]{:S(2)}, u32[]{:S(2)}) collective-permute-start(bf16[3,1792]{1,0:T(4,128)(2,1)} %get-tuple-element.621), channel_id=1, source_target_pairs={{0,1},{1,2},{2,3},{4,5},{5,6},{6,7},{8,9},{9,10},{10,11},{12,13},{... | collective-permute-start | bytes 32264 | tf_op jit(solution)/shard_map/ppermute | solution.py:29
  321.2 47.7 %all-gather.21.cloned.1.call-start = ((), (), s32[]{:S(2)}) async-start(), calls=%async_computation.4 | async-start | bytes 1966080 | tf_op jit(solution)/shard_map/all_gather | solution.py:35
  335.2 25.3 %collective-permute-start.39 = (bf16[8,32,2048]{2,1,0:T(8,128)(2,1)}, bf16[8,32,2048]{2,1,0:T(8,128)(2,1)S(1)}, u32[]{:S(2)}, u32[]{:S(2)}) collective-permute-start(bf16[8,32,2048]{2,1,0:T(8,128)(2,1)} %collective-permute-done.37.refs_1_), channel_id=1, source_target_pairs={{0,1},{1,0},{2,3},{3,2},{4,5},{5,4},{6,7},{7,6},{8,9},{9,8},{10,11... | collective-permute-start | bytes 3145736 | tf_op jit(solution)/shard_map/ppermute | solution.py:376
  335.6 24.9 %collective-permute-start.43 = (bf16[8,32,2048]{2,1,0:T(8,128)(2,1)}, bf16[8,32,2048]{2,1,0:T(8,128)(2,1)}, u32[]{:S(2)}, u32[]{:S(2)}) collective-permute-start(bf16[8,32,2048]{2,1,0:T(8,128)(2,1)} %collective-permute-done.41.refs_5_), channel_id=1, source_target_pairs={{0,1},{1,0},{2,3},{3,2},{4,5},{5,4},{6,7},{7,6},{8,9},{9,8},{10,11... | collective-permute-start | bytes 3145736 | tf_op jit(solution)/shard_map/ppermute | solution.py:376
  345.8 386.9 %all-gather.27.cloned.1.call-start = ((), (), s32[]{:S(2)}) async-start(), calls=%async_computation.7 | async-start | bytes 1966080 | tf_op jit(solution)/shard_map/all_gather | solution.py:59
  532.4 209.3 %all-gather.25.cloned.1.call-start = ((), (), s32[]{:S(2)}) async-start(), calls=%async_computation.6 | async-start | bytes 1966080 | tf_op jit(solution)/shard_map/all_gather | solution.py:59
  601.9 61.7 %collective-permute-start.72 = (bf16[2,2,2,2,64,512]{5,4,3,2,1,0:T(8,128)(2,1)}, bf16[2,2,2,2,64,512]{5,4,3,2,1,0:T(8,128)(2,1)}, u32[]{:S(2)}, u32[]{:S(2)}) collective-permute-start(bf16[2,2,2,2,64,512]{5,4,3,2,1,0:T(8,128)(2,1)} %dynamic-slice_bitcast_fusion.2), channel_id=1, source_target_pairs={{0,1},{1,0},{2,3},{3,2},{4,5},{5,4},{6,7},{7,6},{8,9},{9,8},{10,11... | collective-permute-start | bytes 3145736 | tf_op jit(solution)/shard_map/ppermute | solution.py:376
  604.4 61.1 %collective-permute-start.75 = (bf16[2,2,2,2,64,512]{5,4,1,0,2,3:T(8,128)(2,1)}, bf16[2,2,2,2,64,512]{5,4,1,0,2,3:T(8,128)(2,1)}, u32[]{:S(2)}, u32[]{:S(2)}) collective-permute-start(bf16[2,2,2,2,64,512]{5,4,1,0,2,3:T(8,128)(2,1)} %bitcast.1023), channel_id=1, source_target_pairs={{0,1},{1,0},{2,3},{3,2},{4,5},{5,4},{6,7},{7,6},{8,9},{9,8},{10,11... | collective-permute-start | bytes 3145736 | tf_op jit(solution)/shard_map/ppermute | solution.py:376
  620.5 213.7 %reduce-scatter.5.cloned.1.call-start = ((), (), s32[]{:S(2)}) async-start(), calls=%async_computation.3 | async-start | bytes 655360 | tf_op jit(solution)/shard_map/reduce_scatter | solution.py:365
  626.5 90.0 %collective-permute-start.80 = (bf16[2,2,2,2,32,2048]{5,4,0,1,3,2:T(8,128)(2,1)}, bf16[2,2,2,2,32,2048]{5,4,0,1,3,2:T(8,128)(2,1)}, u32[]{:S(2)}, u32[]{:S(2)}) collective-permute-start(bf16[2,2,2,2,32,2048]{5,4,0,1,3,2:T(8,128)(2,1)} %bitcast.1018), channel_id=1, source_target_pairs={{0,1},{1,0},{2,3},{3,2},{4,5},{5,4},{6,7},{7,6},{8,9},{9,8},{10,11... | collective-permute-start | bytes 6291464 | tf_op jit(solution)/shard_map/ppermute | solution.py:376
  631.5 89.9 %collective-permute-start.83 = (bf16[2,2,2,2,32,2048]{5,4,0,1,2,3:T(8,128)(2,1)}, bf16[2,2,2,2,32,2048]{5,4,0,1,2,3:T(8,128)(2,1)}, u32[]{:S(2)}, u32[]{:S(2)}) collective-permute-start(bf16[2,2,2,2,32,2048]{5,4,0,1,2,3:T(8,128)(2,1)} %bitcast.1017), channel_id=1, source_target_pairs={{0,1},{1,0},{2,3},{3,2},{4,5},{5,4},{6,7},{7,6},{8,9},{9,8},{10,11... | collective-permute-start | bytes 6291464 | tf_op jit(solution)/shard_map/ppermute | solution.py:376
  637.5 31.8 %collective-permute-start.88 = (bf16[2,2,2,2,64,512]{5,4,0,1,3,2:T(8,128)(2,1)}, bf16[2,2,2,2,64,512]{5,4,0,1,3,2:T(8,128)(2,1)}, u32[]{:S(2)}, u32[]{:S(2)}) collective-permute-start(bf16[2,2,2,2,64,512]{5,4,0,1,3,2:T(8,128)(2,1)} %bitcast.1022), channel_id=1, source_target_pairs={{0,1},{1,0},{2,3},{3,2},{4,5},{5,4},{6,7},{7,6},{8,9},{9,8},{10,11... | collective-permute-start | bytes 3145736 | tf_op jit(solution)/shard_map/ppermute | solution.py:376
  643.0 191.2 %reduce-scatter.3.cloned.1.call-start = ((), (), s32[]{:S(2)}) async-start(), calls=%async_computation.2 | async-start | bytes 655360 | tf_op jit(solution)/shard_map/reduce_scatter | solution.py:365
  653.1 327.9 %all-reduce.47.cloned.1.call-start = ((), (), s32[]{:S(2)}) async-start(), calls=%async_computation.8 | async-start | bytes 131072
  671.7 19.5 %collective-permute-start.89 = (bf16[2,2,2,64,512]{4,3,0,1,2:T(8,128)(2,1)S(1)}, bf16[2,2,2,64,512]{4,3,0,1,2:T(8,128)(2,1)S(1)}, u32[]{:S(2)}, u32[]{:S(2)}) collective-permute-start(bf16[2,2,2,64,512]{4,3,0,1,2:T(8,128)(2,1)S(1)} %dynamic-slice_bitcast_fusion.6), channel_id=1, source_target_pairs={{0,4},{1,5},{2,6},{3,7},{4,0},{5,1},{6,2},{7,3},{8,12},{9,13},{10,... | collective-permute-start | bytes 1572872 | tf_op jit(solution)/shard_map/ppermute | solution.py:376
  680.4 17.7 %collective-permute-start.92 = (bf16[2,2,2,64,512]{4,3,0,1,2:T(8,128)(2,1)S(1)}, bf16[2,2,2,64,512]{4,3,0,1,2:T(8,128)(2,1)S(1)}, u32[]{:S(2)}, u32[]{:S(2)}) collective-permute-start(bf16[2,2,2,64,512]{4,3,0,1,2:T(8,128)(2,1)S(1)} %dynamic-slice_bitcast_fusion.5), channel_id=1, source_target_pairs={{0,2},{1,3},{2,0},{3,1},{4,6},{5,7},{6,4},{7,5},{8,10},{9,11},{10,... | collective-permute-start | bytes 1572872 | tf_op jit(solution)/shard_map/ppermute | solution.py:376
  684.1 19.7 %collective-permute-start.74 = (bf16[2,2,64,512]{3,2,1,0:T(8,128)(2,1)S(1)}, bf16[2,2,64,512]{3,2,1,0:T(8,128)(2,1)S(1)}, u32[]{:S(2)}, u32[]{:S(2)}) collective-permute-start(bf16[2,2,64,512]{3,2,1,0:T(8,128)(2,1)S(1)} %dynamic-slice_bitcast_fusion.19), channel_id=1, source_target_pairs={{0,2},{1,3},{2,0},{3,1},{4,6},{5,7},{6,4},{7,5},{8,10},{9,11},{10,... | collective-permute-start | bytes 786440 | tf_op jit(solution)/shard_map/ppermute | solution.py:376
  710.5 15.4 %collective-permute-start.94 = (bf16[2,2,64,512]{3,2,0,1:T(8,128)(2,1)S(1)}, bf16[2,2,64,512]{3,2,0,1:T(8,128)(2,1)S(1)}, u32[]{:S(2)}, u32[]{:S(2)}) collective-permute-start(bf16[2,2,64,512]{3,2,0,1:T(8,128)(2,1)S(1)} %fusion.251), channel_id=1, source_target_pairs={{0,8},{1,9},{2,10},{3,11},{4,12},{5,13},{6,14},{7,15},{8,0},{9,1},... | collective-permute-start | bytes 786440 | tf_op jit(solution)/shard_map/ppermute | solution.py:376
  720.0 266.3 %collective-permute-start.81 = (bf16[2,2,2,32,2048]{4,3,0,1,2:T(8,128)(2,1)}, bf16[2,2,2,32,2048]{4,3,0,1,2:T(8,128)(2,1)}, u32[]{:S(2)}, u32[]{:S(2)}) collective-permute-start(bf16[2,2,2,32,2048]{4,3,0,1,2:T(8,128)(2,1)} %dynamic-slice_bitcast_fusion.1), channel_id=1, source_target_pairs={{0,4},{1,5},{2,6},{3,7},{4,0},{5,1},{6,2},{7,3},{8,12},{9,13},{10,... | collective-permute-start | bytes 3145736 | tf_op jit(solution)/shard_map/ppermute | solution.py:376
  725.2 263.0 %collective-permute-start.84 = (bf16[2,2,2,32,2048]{4,3,0,1,2:T(8,128)(2,1)}, bf16[2,2,2,32,2048]{4,3,0,1,2:T(8,128)(2,1)}, u32[]{:S(2)}, u32[]{:S(2)}) collective-permute-start(bf16[2,2,2,32,2048]{4,3,0,1,2:T(8,128)(2,1)} %dynamic-slice_bitcast_fusion), channel_id=1, source_target_pairs={{0,2},{1,3},{2,0},{3,1},{4,6},{5,7},{6,4},{7,5},{8,10},{9,11},{10,... | collective-permute-start | bytes 3145736 | tf_op jit(solution)/shard_map/ppermute | solution.py:376
  784.3 47.2 %collective-permute-start.55 = (f32[3,1792]{1,0:T(4,128)S(1)}, f32[3,1792]{1,0:T(4,128)S(1)}, u32[]{:S(2)}, u32[]{:S(2)}) collective-permute-start(f32[3,1792]{1,0:T(4,128)S(1)} %pad_add_fusion.2), channel_id=1, source_target_pairs={{1,0},{2,1},{3,2},{5,4},{6,5},{7,6},{9,8},{10,9},{11,10},{13,12},{... | collective-permute-start | bytes 64520 | tf_op jit(solution)/shard_map/ppermute | solution.py:29
  865.5 125.9 %collective-permute-start.56 = (bf16[2,2,2,2,32,768]{5,4,0,1,3,2:T(8,128)(2,1)}, bf16[2,2,2,2,32,768]{5,4,0,1,3,2:T(8,128)(2,1)}, u32[]{:S(2)}, u32[]{:S(2)}) collective-permute-start(bf16[2,2,2,2,32,768]{5,4,0,1,3,2:T(8,128)(2,1)} %bitcast.1025), channel_id=1, source_target_pairs={{0,1},{1,0},{2,3},{3,2},{4,5},{5,4},{6,7},{7,6},{8,9},{9,8},{10,11... | collective-permute-start | bytes 2359304 | tf_op jit(solution)/shard_map/ppermute | solution.py:376
  868.6 125.2 %collective-permute-start.59 = (bf16[2,2,2,2,32,768]{5,4,0,1,2,3:T(8,128)(2,1)}, bf16[2,2,2,2,32,768]{5,4,0,1,2,3:T(8,128)(2,1)}, u32[]{:S(2)}, u32[]{:S(2)}) collective-permute-start(bf16[2,2,2,2,32,768]{5,4,0,1,2,3:T(8,128)(2,1)} %bitcast.1024), channel_id=1, source_target_pairs={{0,1},{1,0},{2,3},{3,2},{4,5},{5,4},{6,7},{7,6},{8,9},{9,8},{10,11... | collective-permute-start | bytes 2359304 | tf_op jit(solution)/shard_map/ppermute | solution.py:376
  870.7 151.1 %collective-permute-start.64 = (bf16[2,2,2,2,32,1408]{5,4,0,1,3,2:T(8,128)(2,1)}, bf16[2,2,2,2,32,1408]{5,4,0,1,3,2:T(8,128)(2,1)}, u32[]{:S(2)}, u32[]{:S(2)}) collective-permute-start(bf16[2,2,2,2,32,1408]{5,4,0,1,3,2:T(8,128)(2,1)} %bitcast.1020), channel_id=1, source_target_pairs={{0,1},{1,0},{2,3},{3,2},{4,5},{5,4},{6,7},{7,6},{8,9},{9,8},{10,11... | collective-permute-start | bytes 4325384 | tf_op jit(solution)/shard_map/ppermute | solution.py:376
  986.3 38.2 %collective-permute-start.67 = (bf16[2,2,2,2,32,1408]{5,4,0,1,2,3:T(8,128)(2,1)}, bf16[2,2,2,2,32,1408]{5,4,0,1,2,3:T(8,128)(2,1)S(1)}, u32[]{:S(2)}, u32[]{:S(2)}) collective-permute-start(bf16[2,2,2,2,32,1408]{5,4,0,1,2,3:T(8,128)(2,1)} %bitcast.1129), channel_id=1, source_target_pairs={{0,1},{1,0},{2,3},{3,2},{4,5},{5,4},{6,7},{7,6},{8,9},{9,8},{10,11... | collective-permute-start | bytes 4325384 | tf_op jit(solution)/shard_map/ppermute | solution.py:376
  988.2 24.3 %collective-permute-start.82 = (bf16[2,2,32,2048]{3,2,0,1:T(8,128)(2,1)S(1)}, bf16[2,2,32,2048]{3,2,0,1:T(8,128)(2,1)S(1)}, u32[]{:S(2)}, u32[]{:S(2)}) collective-permute-start(bf16[2,2,32,2048]{3,2,0,1:T(8,128)(2,1)S(1)} %dynamic-slice_bitcast_fusion.8), channel_id=1, source_target_pairs={{0,2},{1,3},{2,0},{3,1},{4,6},{5,7},{6,4},{7,5},{8,10},{9,11},{10,... | collective-permute-start | bytes 1572872 | tf_op jit(solution)/shard_map/ppermute | solution.py:376
  995.2 15.7 %collective-permute-start.60 = (bf16[2,2,2,32,768]{4,3,0,1,2:T(8,128)(2,1)S(1)}, bf16[2,2,2,32,768]{4,3,0,1,2:T(8,128)(2,1)S(1)}, u32[]{:S(2)}, u32[]{:S(2)}) collective-permute-start(bf16[2,2,2,32,768]{4,3,0,1,2:T(8,128)(2,1)S(1)} %dynamic-slice_bitcast_fusion.11), channel_id=1, source_target_pairs={{0,2},{1,3},{2,0},{3,1},{4,6},{5,7},{6,4},{7,5},{8,10},{9,11},{10,... | collective-permute-start | bytes 1179656 | tf_op jit(solution)/shard_map/ppermute | solution.py:376
  1019.1 23.7 %collective-permute-start.86 = (bf16[2,2,32,2048]{3,2,0,1:T(8,128)(2,1)S(1)}, bf16[2,2,32,2048]{3,2,0,1:T(8,128)(2,1)S(1)}, u32[]{:S(2)}, u32[]{:S(2)}) collective-permute-start(bf16[2,2,32,2048]{3,2,0,1:T(8,128)(2,1)S(1)} %fusion.215), channel_id=1, source_target_pairs={{0,8},{1,9},{2,10},{3,11},{4,12},{5,13},{6,14},{7,15},{8,0},{9,1},... | collective-permute-start | bytes 1572872 | tf_op jit(solution)/shard_map/ppermute | solution.py:376
  1023.7 28.5 %collective-permute-start.65 = (bf16[2,2,2,32,1408]{4,3,0,1,2:T(8,128)(2,1)S(1)}, bf16[2,2,2,32,1408]{4,3,0,1,2:T(8,128)(2,1)S(1)}, u32[]{:S(2)}, u32[]{:S(2)}) collective-permute-start(bf16[2,2,2,32,1408]{4,3,0,1,2:T(8,128)(2,1)S(1)} %dynamic-slice_bitcast_fusion.4), channel_id=1, source_target_pairs={{0,4},{1,5},{2,6},{3,7},{4,0},{5,1},{6,2},{7,3},{8,12},{9,13},{10,... | collective-permute-start | bytes 2162696 | tf_op jit(solution)/shard_map/ppermute | solution.py:376
  1035.8 17.2 %collective-permute-start.68 = (bf16[2,2,2,32,1408]{4,3,0,1,2:T(8,128)(2,1)S(1)}, bf16[2,2,2,32,1408]{4,3,0,1,2:T(8,128)(2,1)S(1)}, u32[]{:S(2)}, u32[]{:S(2)}) collective-permute-start(bf16[2,2,2,32,1408]{4,3,0,1,2:T(8,128)(2,1)S(1)} %dynamic-slice_bitcast_fusion.3), channel_id=1, source_target_pairs={{0,2},{1,3},{2,0},{3,1},{4,6},{5,7},{6,4},{7,5},{8,10},{9,11},{10,... | collective-permute-start | bytes 2162696 | tf_op jit(solution)/shard_map/ppermute | solution.py:376
  (390 other events, 3721.4 us)
Sparse Core Ops, SparseCore 0:
  321.3 19.9 all-gather.22
  346.0 19.9 all-gather.20
  532.5 49.7 all-gather.26
  620.6 19.7 all-gather.24
  643.3 21.2 reduce-scatter.4
  667.1 24.5 reduce-scatter.2
  861.4 119.5 all-reduce.46
